TPU v7x, 256 devices: a whole 4x4x8 slice. The times are simulated.
256 devices in a mesh: lx: 16 (over y_hi, z), ly: 16 (over y_lo, x, core).
Axes of the slice: x: 4, y: 4 (y_hi: 2, y_lo: 2; y = y_hi * 2 + y_lo), z: 8, core: 2. Of those that a mesh axis runs over, the one named last changes fastest.
Arguments:
- site_tensor: bfloat16 [16, 16, 4, 3, 3, 3, 3], P('lx', 'ly'), may hold values from -4 to 4
- phys_charge: int32 [16, 16, 4], P('lx', 'ly'), may hold values from 0 to 2
- virt_charge: int32 [16, 16, 4, 3], P('lx', 'ly'), may hold values from 0 to 2
- env_charge: int32 [16, 16, 2, 128], P('lx', 'ly'), may hold values from 0 to 3
- corner_ul: bfloat16 [16, 16, 128, 128], P('lx', 'ly'), may hold values from -0.5 to 0.5
- corner_ur: bfloat16 [16, 16, 128, 128], P('lx', 'ly'), may hold values from -0.5 to 0.5
- corner_ll: bfloat16 [16, 16, 128, 128], P('lx', 'ly'), may hold values from -0.5 to 0.5
- edge_top: bfloat16 [16, 16, 128, 9, 128], P('lx', 'ly'), may hold values from -0.5 to 0.5
- edge_right: bfloat16 [16, 16, 128, 9, 128], P('lx', 'ly'), may hold values from -0.5 to 0.5
- edge_bottom: bfloat16 [16, 16, 128, 9, 128], P('lx', 'ly'), may hold values from -0.5 to 0.5
- edge_left: bfloat16 [16, 16, 128, 9, 128], P('lx', 'ly'), may hold values from -0.5 to 0.5
- sketch: bfloat16 [16, 16, 4, 1152, 128], P('lx', 'ly'), may hold values from -6 to 6
Outputs:
- left_upper_corner: bfloat16 [16, 16, 128, 128], P('lx', 'ly')
- left_edge_new: bfloat16 [16, 16, 128, 9, 128], P('lx', 'ly')
- left_lower_corner: bfloat16 [16, 16, 128, 128], P('lx', 'ly')
- top_left_corner: bfloat16 [16, 16, 128, 128], P('lx', 'ly')
- top_edge_new: bfloat16 [16, 16, 128, 9, 128], P('lx', 'ly')
- top_right_corner: bfloat16 [16, 16, 128, 128], P('lx', 'ly')
All inputs are finite; a program needn't handle non-finite values.
Results may differ from a plain program's by a relative error of at most 0.013.
Values may be sent and summed in bfloat16 or wider, within the bound.
No kernel may reach another device: no remote copies, remote signals or barrier semaphores. Data moves between devices by JAX's collectives and lax.ppermute only.
A program may use at most 128 MiB of HBM per device.

v0:
```python
import functools

import jax
import jax.numpy as jnp
from jax import lax
from jax.experimental import pallas as pl
from jax.experimental.pallas import tpu as pltpu
from jax.sharding import PartitionSpec as P

F32 = jnp.float32
BF16 = jnp.bfloat16
CHI = 128
D2 = 9
PAD = 16
CUT = CHI * D2
TALL = CHI * PAD
LAY = D2 * PAD
GROUP = 16
CHUNKS = CHI // GROUP
ROWS = GROUP * PAD
VMEM = 56 * 1024 * 1024


def dot(a, b):
    return lax.dot_general(a, b, (((1,), (0,)), ((), ())), preferred_element_type=F32)


def dot_nt(a, b):
    return lax.dot_general(a, b, (((1,), (1,)), ((), ())), preferred_element_type=F32)


def dot_tn(a, b):
    return lax.dot_general(a, b, (((0,), (0,)), ((), ())), preferred_element_type=F32)


def exact_tn(a, b):
    return lax.dot_general(
        a, b, (((0,), (0,)), ((), ())), precision=lax.Precision.HIGHEST, preferred_element_type=F32
    )


def exact_nt(a, b):
    return lax.dot_general(
        a, b, (((1,), (1,)), ((), ())), precision=lax.Precision.HIGHEST, preferred_element_type=F32
    )


def slab(ref, p):
    return ref[p * CHI : (p + 1) * CHI, :]


def side_by_side(ref):
    return jnp.concatenate([slab(ref, p) for p in range(D2)], axis=1)


def spread_rows(slab_of, wide):
    wide[...] = jnp.zeros_like(wide)
    for p in range(D2):
        wide[pl.ds(p, CHI, stride=PAD), :] = slab_of(p).astype(F32)
    return wide[...].astype(BF16)


def gathered_row(wide, p):
    return wide[pl.ds(p, CHI, stride=PAD), :]


def chain(left, right, layer, consume):
    for chunk in range(CHUNKS):
        rows = pl.ds(chunk * ROWS, ROWS)
        three = dot(left[rows, :], right[...]).astype(BF16)
        stacked = jnp.concatenate(
            [
                jnp.concatenate(
                    [
                        three[f * PAD : (f + 1) * PAD, q * CHI : (q + 1) * CHI]
                        for q in range(D2)
                    ],
                    axis=0,
                )
                for f in range(GROUP)
            ],
            axis=1,
        )
        mixed = dot(layer[...], stacked).astype(BF16)
        consume(
            chunk,
            jnp.concatenate(
                [
                    jnp.concatenate(
                        [
                            mixed[s * PAD : (s + 1) * PAD, f * CHI : (f + 1) * CHI]
                            for s in range(D2)
                        ],
                        axis=1,
                    )
                    for f in range(GROUP)
                ],
                axis=0,
            ),
        )


def third(n):
    return (n * 11) >> 5


def layer_masks():
    row = lax.broadcasted_iota(jnp.int32, (LAY, 81), 0)
    lane = lax.broadcasted_iota(jnp.int32, (LAY, 81), 1)
    slow, fast = row >> 4, row & 15
    valid = fast < D2
    pairs = ((third(slow), third(fast)), (slow - 3 * third(slow), fast - 3 * third(fast)))
    leg_l = (lane * 19) >> 9
    rest = lane - 27 * leg_l
    leg_u = (rest * 57) >> 9
    rest = rest - 9 * leg_u
    leg_r = (rest * 11) >> 5
    leg_d = rest - 3 * leg_r

    def mask(slow_leg, fast_leg):
        return [
            jnp.where(valid & (slow_leg == a) & (fast_leg == b), 1.0, 0.0).astype(F32)
            for a, b in pairs
        ]

    return mask(leg_r, leg_u), mask(leg_d, leg_l), mask(leg_r, leg_d), mask(leg_u, leg_l)


def kept_rows(site, phys, virt):
    lane = lax.broadcasted_iota(jnp.int32, (4, 81), 1)
    state = lax.broadcasted_iota(jnp.int32, (4, 81), 0)
    leg_l = (lane * 19) >> 9
    rest = lane - 27 * leg_l
    leg_u = (rest * 57) >> 9
    rest = rest - 9 * leg_u
    leg_r = (rest * 11) >> 5
    leg_d = rest - 3 * leg_r
    total = jnp.zeros((4, 81), jnp.int32)
    for s in range(4):
        total = total + jnp.where(state == s, phys[s], 0)
    for i in range(3):
        total = total + jnp.where(leg_l == i, virt[0, i], 0)
        total = total + jnp.where(leg_u == i, virt[1, i], 0)
        total = total - jnp.where(leg_r == i, virt[2, i], 0)
        total = total - jnp.where(leg_d == i, virt[3, i], 0)
    return jnp.where(total == 0, site[...].astype(F32), 0.0)


def build_layers(kept, out_a, out_b, out_c):
    m_ru, m_dl, m_rd, m_ul = layer_masks()

    def build(rows, cols):
        halves = []
        for half in range(2):
            tall = jnp.concatenate([rows[half] * kept[s : s + 1, :] for s in range(4)], axis=0)
            halves.append(dot_nt(tall.astype(BF16), cols[half].astype(BF16)))
        ket_bra = halves[0] * halves[1]
        total = ket_bra[:LAY]
        for s in range(1, 4):
            total = total + ket_bra[s * LAY : (s + 1) * LAY]
        return total.astype(BF16)

    out_a[...] = build(m_dl, m_ru)
    out_b[...] = build(m_ru, m_dl)
    out_c[...] = build(m_rd, m_ul)


def right_kernel(
    phys, virt, site, corner, edge_r, edge_t, sketch, term, lay_a, lay_b, lay_c, pair_out, wide_t, wide
):
    build_layers(kept_rows(site, phys, virt), lay_a, lay_b, lay_c)
    pair_out[...] = dot(corner[...], side_by_side(edge_r)).astype(BF16)
    wide_t[...] = spread_rows(lambda p: slab(edge_t, p), wide)

    def consume(chunk, block):
        wide[pl.ds(chunk * ROWS, ROWS), :] = dot(block, sketch[...])

    chain(wide_t, pair_out, lay_a, consume)
    for p in range(D2):
        term[p * CHI : (p + 1) * CHI, :] = gathered_row(wide, p).astype(term.dtype)


def lower_kernel(corner, edge_b, edge_l, sketch, lay_b, term, pair_out, wide_l, wide):
    pair_out[...] = dot(corner[...], side_by_side(edge_b)).astype(BF16)
    wide_l[...] = spread_rows(lambda p: slab(edge_l, p), wide)

    def consume(chunk, block):
        wide[pl.ds(chunk * ROWS, ROWS), :] = dot(block, sketch[...])

    chain(wide_l, pair_out, lay_b, consume)
    for p in range(D2):
        term[p * CHI : (p + 1) * CHI, :] = gathered_row(wide, p).astype(term.dtype)


def upper_kernel(
    corner, edge_t, edge_l, sketch_l, sketch_t, lay_c,
    own_left, own_top, corner_edge, corner_side,
    left_rows, sketch_cols, sketch_rows, wide, top_sum,
):
    corner_edge[...] = dot(corner[...], side_by_side(edge_t)).astype(BF16)
    corner_side[...] = dot_tn(corner[...], side_by_side(edge_l)).astype(BF16)
    left_rows[...] = spread_rows(lambda p: jnp.transpose(slab(edge_l, p).astype(F32)), wide)
    wide[0:CUT, :] = sketch_l[...].astype(F32)
    for p in range(D2):
        sketch_cols[p * CHI : (p + 1) * CHI, :] = wide[pl.ds(p, CHI, stride=D2), :].astype(BF16)
    wide[0:CUT, :] = sketch_t[...].astype(F32)
    picked = [wide[pl.ds(p, CHI, stride=D2), :] for p in range(D2)]
    sketch_rows[...] = spread_rows(lambda p: picked[p], wide)
    top_sum[...] = jnp.zeros_like(top_sum)

    def consume(chunk, block):
        rows = pl.ds(chunk * ROWS, ROWS)
        wide[rows, :] = dot(block, sketch_cols[...])
        top_sum[...] += dot_tn(sketch_rows[rows, :], block)

    chain(left_rows, corner_edge, lay_c, consume)
    for p in range(D2):
        own_left[p * CHI : (p + 1) * CHI, :] = gathered_row(wide, p)
        own_top[p * CHI : (p + 1) * CHI, :] = jnp.transpose(top_sum[:, p * CHI : (p + 1) * CHI])


BLOCK = 32


def eliminate(grams):
    count = len(grams)
    row = lax.broadcasted_iota(jnp.int32, (CHI, CHI), 0)
    col = lax.broadcasted_iota(jnp.int32, (CHI, CHI), 1)
    eye = jnp.where(row == col, 1.0, 0.0).astype(F32)
    both = [jnp.concatenate([g, eye], axis=1) for g in grams]
    done = [[] for _ in grams]
    in_row = lax.broadcasted_iota(jnp.int32, (BLOCK, 1), 0)
    for start in range(0, CHI, BLOCK):
        panels = [b[:BLOCK] for b in both]
        roots = [jnp.zeros((BLOCK, 1), F32) for _ in grams]
        for j in range(BLOCK):
            for m in range(count):
                panel = panels[m]
                column = panel[:, start + j : start + j + 1]
                pivot = column[j : j + 1, :]
                scale = jnp.where(in_row > j, column * (1.0 / pivot), 0.0)
                roots[m] = jnp.where(in_row == j, lax.rsqrt(pivot), roots[m])
                panels[m] = panel - scale * panel[j : j + 1, :]
        for m in range(count):
            panels[m] = panels[m] * roots[m]
            done[m].append(panels[m][:, CHI:])
            if start + BLOCK < CHI:
                across = panels[m][:, :CHI]
                update = exact_tn(across, panels[m])[start + BLOCK :]
                both[m] = both[m][BLOCK:] - update
    return [jnp.concatenate(d, axis=0) for d in done]


def basis_kernel(virt, env, own_left, below, own_top, beside, left_out, top_out, range_l, range_t):
    row = lax.broadcasted_iota(jnp.int32, (CHI, CHI), 0)
    col = lax.broadcasted_iota(jnp.int32, (CHI, CHI), 1)
    grams = []
    for side, (own, other, ranged, leg) in enumerate(
        ((own_left, below, range_l, 3), (own_top, beside, range_t, 2))
    ):
        across = jnp.broadcast_to(env[side : side + 1, :].astype(F32), (CHI, CHI))
        gap = across - jnp.transpose(across)
        for p in range(D2):
            shift = (virt[leg, p // 3] - virt[leg, p % 3]).astype(F32)
            total = slab(own, p) + slab(other, p).astype(F32)
            ranged[p * CHI : (p + 1) * CHI, :] = jnp.where(gap == shift, total, 0.0)
        gram = exact_tn(ranged[...], ranged[...])
        diagonal = jnp.where(row == col, gram, 0.0)
        mean = jnp.sum(jnp.sum(diagonal, axis=1, keepdims=True), axis=0, keepdims=True) / CHI
        grams.append(gram + jnp.where(row == col, 0.01 * mean + 1e-06, 0.0))
    inverses = eliminate(grams)
    left_out[...] = exact_nt(range_l[...], inverses[0]).astype(BF16)
    top_out[...] = exact_nt(range_t[...], inverses[1]).astype(BF16)


def unit(values):
    square = jnp.sum(jnp.sum(values * values, axis=1, keepdims=True), axis=0, keepdims=True)
    return (values / jnp.sqrt(square / values.size + 1e-06)).astype(BF16)


def slab_rows(wide_ref, p):
    return wide_ref[:, p * CHI : (p + 1) * CHI]


def corner_from(projector, pair):
    tall = jnp.concatenate([slab_rows(pair, p) for p in range(D2)], axis=0)
    return dot_tn(projector[...], tall)


def final_kernel(
    left, top, above, before, wide_l, wide_t, lay_a, lay_b, corner_edge, corner_side, lower_pair, right_pair,
    out_lu, out_le, out_ll, out_tl, out_te, out_tr,
    beside, spread, wide, total,
):
    out_ll[...] = unit(corner_from(left, lower_pair))
    out_tr[...] = unit(corner_from(top, right_pair))
    out_lu[...] = unit(corner_from(above, corner_edge))
    out_tl[...] = unit(jnp.transpose(corner_from(before, corner_side)))
    for own, other, natural, layer, out in (
        (left, above, wide_l, lay_b, out_le),
        (top, before, wide_t, lay_a, out_te),
    ):
        beside[...] = side_by_side(own)
        spread[...] = spread_rows(lambda p: slab(other, p), wide)
        total[...] = jnp.zeros_like(total)

        def consume(chunk, block):
            total[...] += dot_tn(spread[pl.ds(chunk * ROWS, ROWS), :], block)

        chain(natural, beside, layer, consume)
        result = unit(total[...])
        for p in range(D2):
            out[p * CHI : (p + 1) * CHI, :] = result[:, p * CHI : (p + 1) * CHI]


def shape(*dims, dtype=BF16):
    return jax.ShapeDtypeStruct(dims, dtype)


def vmem_in(count):
    return [pl.BlockSpec(memory_space=pltpu.VMEM)] * count


def smem_in(count):
    return [pl.BlockSpec(memory_space=pltpu.SMEM)] * count


def call(body, name, smem, ins, outs, scratch, flops):
    moved = sum(a.size * a.dtype.itemsize for a in ins) + sum(
        o.size * jnp.dtype(o.dtype).itemsize for o in outs
    )
    return pl.pallas_call(
        body,
        name=name,
        out_shape=tuple(outs),
        in_specs=smem_in(len(smem)) + vmem_in(len(ins)),
        out_specs=tuple(vmem_in(len(outs))),
        scratch_shapes=[pltpu.VMEM(s, d) for s, d in scratch],
        compiler_params=pltpu.CompilerParams(vmem_limit_bytes=VMEM),
        cost_estimate=pl.CostEstimate(flops=flops, bytes_accessed=moved, transcendentals=0),
    )(*smem, *ins)


def from_behind(block, axis, distance):
    size = lax.axis_size(axis)
    route = [((i - distance) % size, i) for i in range(size)]
    return lax.ppermute(block, axis, route)


SEND = BF16


def flat(edge):
    return edge.transpose(1, 0, 2).reshape(CUT, CHI)


def shards(
    site_tensor, phys_charge, virt_charge, env_charge, corner_ul, corner_ur, corner_ll,
    edge_top, edge_right, edge_bottom, edge_left, sketch,
):
    site = site_tensor[0, 0].reshape(4, 81)
    phys, virt, env = phys_charge[0, 0], virt_charge[0, 0], env_charge[0, 0]
    ul, ur, ll = corner_ul[0, 0], corner_ur[0, 0], corner_ll[0, 0]
    top, right, bottom, left = (
        flat(e[0, 0]) for e in (edge_top, edge_right, edge_bottom, edge_left)
    )
    sketches = [sketch[0, 0, i] for i in range(4)]
    tall = shape(CUT, CHI)
    broad = shape(CHI, CUT)
    lay = shape(LAY, LAY)
    padded = shape(TALL, CHI)
    wide = ((TALL, CHI), F32)
    work = 1_000_000_000
    from_right, lay_a, lay_b, lay_c, right_pair, wide_t = call(
        right_kernel, "right", [phys, virt], [site, ur, right, top, sketches[3]],
        [shape(CUT, CHI, dtype=SEND), lay, lay, lay, broad, padded], [wide], work,
    )
    beside = from_behind(from_right, "lx", -1)
    from_lower, lower_pair, wide_l = call(
        lower_kernel, "lower", [], [ll, bottom, left, sketches[1], lay_b],
        [shape(CUT, CHI, dtype=SEND), broad, padded], [wide], work,
    )
    below = from_behind(from_lower, "ly", -1)
    own_left, own_top, corner_edge, corner_side = call(
        upper_kernel, "upper", [], [ul, top, left, sketches[0], sketches[2], lay_c],
        [shape(CUT, CHI, dtype=F32), shape(CUT, CHI, dtype=F32), broad, broad],
        [((TALL, CHI), BF16), ((CUT, CHI), BF16), ((TALL, CHI), BF16), wide, ((CHI, CUT), F32)], work,
    )
    left_basis, top_basis = call(
        basis_kernel, "basis", [virt], [env, own_left, below, own_top, beside], [tall, tall],
        [((CUT, CHI), F32), ((CUT, CHI), F32)], work,
    )
    before = from_behind(top_basis, "lx", 1)
    above = from_behind(left_basis, "ly", 1)
    corner = shape(CHI, CHI)
    lu, le, lo, tl, te, tr = call(
        final_kernel, "final", [],
        [left_basis, top_basis, above, before, wide_l, wide_t, lay_a, lay_b,
         corner_edge, corner_side, lower_pair, right_pair],
        [corner, tall, corner, corner, tall, corner],
        [((CHI, CUT), BF16), ((TALL, CHI), BF16), wide, ((CHI, CUT), F32)], work,
    )
    lift = lambda a: a[None, None]
    edge = lambda a: a.reshape(D2, CHI, CHI).transpose(1, 0, 2)[None, None]
    return lift(lu), edge(le), lift(lo), lift(tl), edge(te), lift(tr)


def solution(mesh):
    split = lambda rest: P("lx", "ly", *([None] * rest))
    in_specs = tuple(split(rest) for rest in (5, 1, 2, 2, 2, 2, 2, 3, 3, 3, 3, 3))
    out_specs = tuple(split(rest) for rest in (2, 3, 2, 2, 3, 2))
    return jax.shard_map(shards, mesh=mesh, in_specs=in_specs, out_specs=out_specs, check_vma=False)
```

profile of v0, /device:TPU:8, one launch (start us, length us, event | category | flops | bytes accessed | tf_op | source)
XLA Modules:
  0.0 86.6 jit_solution(12922151276297298216)
XLA Ops:
  0.6 0.0 copy-start.1
  0.6 0.0 copy-start
  0.7 2.3 %slice_bitcast_fusion = (bf16[1152,128]{1,0:T(8,128)(2,1)}, bf16[1152,128]{1,0:T(8,128)(2,1)}, bf16[1152,128]{1,0:T(8,128)(2,1)}, bf16[1152,128]{1,0:T(8,128)(2,1)}) fusion(bf16[1,1,4,1152,128]{4,3,2,1,0:T(8,128)(2,1)} %param.23), kind=kLoop, calls=%fused_computation | loop fusion | bytes 2359296 | tf_op jit(solution)/shard_map/squeeze | solution.py:367
  2.9 0.0 copy-done.1
  2.9 0.7 copy.20
  3.6 0.7 reshape_squeeze.3.site
  4.3 8.0 %right.1 = (bf16[1152,128]{1,0:T(8,128)(2,1)}, bf16[144,144]{1,0:T(8,128)(2,1)}, bf16[144,144]{1,0:T(8,128)(2,1)}, bf16[144,144]{1,0:T(8,128)(2,1)}, bf16[128,11...) custom-call(s32[4]{0:T(128)} %bitcast.60, s32[4,3]{1,0:T(4,128)} %bitcast.48, bf16[4,81]{1,0:T(4,128)(2,1)} %reshape_squeeze.3.site, ...), custom_call_target="tpu_custom_call" | custom-call | flops 1000000000 | bytes 2156680 | tf_op jit(solution)/shard_map/right/pallas_call | solution.py:332
  12.3 7.4 %lower.1 = (bf16[1152,128]{1,0:T(8,128)(2,1)}, bf16[128,1152]{1,0:T(8,128)(2,1)}, bf16[2048,128]{1,0:T(8,128)(2,1)}) custom-call(bf16[128,128]{1,0:T(8,128)(2,1)} %bitcast.57, bf16[1152,128]{1,0:T(8,128)(2,1)} %bitcast.51, bf16[1152,128]{1,0:T(8,128)(2,1)} %bitcast.54, bf16[1152,128]{1,0:T(8,128)(2,1)} %get-tuple-element.48.sketch, ...), custom_call_target="tpu_custom_call" | custom-call | flops 1000000000 | bytes 2073088 | tf_op jit(solution)/shard_map/lower/pallas_call | solution.py:332
  19.7 2.1 %collective-permute-start = (bf16[1152,128]{1,0:T(8,128)(2,1)}, bf16[1152,128]{1,0:T(8,128)(2,1)S(1)}, u32[]{:S(2)}, u32[]{:S(2)}) collective-permute-start(bf16[1152,128]{1,0:T(8,128)(2,1)} %get-tuple-element.30), channel_id=1, source_target_pairs={{1,0},{2,1},{3,2},{4,3},{5,4},{6,5},{7,6},{8,7},{9,8},{10,9},{11,1... | collective-permute-start | bytes 884744 | tf_op jit(solution)/shard_map/ppermute | solution.py:347
  21.7 0.0 copy-done.2
  21.7 7.9 %collective-permute-start.1 = (bf16[1152,128]{1,0:T(8,128)(2,1)S(1)}, bf16[1152,128]{1,0:T(8,128)(2,1)S(1)}, u32[]{:S(2)}, u32[]{:S(2)}) collective-permute-start(bf16[1152,128]{1,0:T(8,128)(2,1)S(1)} %copy-done.2), channel_id=1, source_target_pairs={{16,0},{32,16},{48,32},{64,48},{80,64},{96,80},{112,96},{128,112},... | collective-permute-start | bytes 884744 | tf_op jit(solution)/shard_map/ppermute | solution.py:347
  29.6 9.3 %upper.1 = (f32[1152,128]{1,0:T(8,128)}, f32[1152,128]{1,0:T(8,128)}, bf16[128,1152]{1,0:T(8,128)(2,1)}, bf16[128,1152]{1,0:T(8,128)(2,1)}) custom-call(bf16[128,128]{1,0:T(8,128)(2,1)} %bitcast.58, bf16[1152,128]{1,0:T(8,128)(2,1)} %bitcast.53, bf16[1152,128]{1,0:T(8,128)(2,1)} %bitcast.55, bf16[1152,128]{1,0:T(8,128)(2,1)} %get-tuple-element.50.sketch_l, ...), custom_call_target="tpu_custom_call" | custom-call | flops 1000000000 | bytes 3023360 | tf_op jit(solution)/shard_map/upper/pallas_call | solution.py:332
  39.0 0.0 collective-permute-done.below
  39.0 0.0 collective-permute-done.1.beside
  39.0 0.0 copy-start.6
  39.0 0.7 copy-done.5
  39.7 0.1 copy-done.6
  39.8 17.5 %basis.1 = (bf16[1152,128]{1,0:T(8,128)(2,1)}, bf16[1152,128]{1,0:T(8,128)(2,1)}) custom-call(s32[4,3]{1,0:T(4,128)} %bitcast.49, s32[2,128]{1,0:T(2,128)} %bitcast.59, f32[1152,128]{1,0:T(8,128)} %get-tuple-element.28.own_left, bf16[1152,128]{1,0:T(8,128)(2,1)} %copy-done.5, f32[1152,128]{1,0:T(8,128)} %get-tuple-element.31.own_top, bf16[1152,128]{1,0:T(8,128)(2,1)} %copy-done.6), custom_call_target="tpu_custom_call" | custom-call | flops 1000000000 | bytes 2360320 | tf_op jit(solution)/shard_map/basis/pallas_call | solution.py:332
  57.3 0.0 collective-permute-start.2
  57.3 0.0 collective-permute-start.3
  57.3 11.6 %collective-permute-done.2.above = bf16[1152,128]{1,0:T(8,128)(2,1)S(1)} collective-permute-done((bf16[1152,128]{1,0:T(8,128)(2,1)}, bf16[1152,128]{1,0:T(8,128)(2,1)S(1)}, u32[]{:S(2)}, u32[]{:S(2)}) %collective-permute-start.2) | collective-permute-done | bytes 294944 | tf_op jit(solution)/shard_map/ppermute | solution.py:347
  68.9 3.0 %collective-permute-done.3.before = bf16[1152,128]{1,0:T(8,128)(2,1)S(1)} collective-permute-done((bf16[1152,128]{1,0:T(8,128)(2,1)}, bf16[1152,128]{1,0:T(8,128)(2,1)S(1)}, u32[]{:S(2)}, u32[]{:S(2)}) %collective-permute-start.3) | collective-permute-done | bytes 294944 | tf_op jit(solution)/shard_map/ppermute | solution.py:347
  72.0 0.7 copy-done.4
  72.7 13.9 %final.1 = (bf16[128,128]{1,0:T(8,128)(2,1)}, bf16[1152,128]{1,0:T(8,128)(2,1)}, bf16[128,128]{1,0:T(8,128)(2,1)}, bf16[128,128]{1,0:T(8,128)(2,1)}, bf16[1152,1...) custom-call(bf16[1152,128]{1,0:T(8,128)(2,1)} %get-tuple-element.33.left, bf16[1152,128]{1,0:T(8,128)(2,1)} %get-tuple-element.34.top, ...), custom_call_target="tpu_custom_call" | custom-call | flops 1000000000 | bytes 4211712 | tf_op jit(solution)/shard_map/final/pallas_call | solution.py:332
  (7 shorter events, 0.0 us)
Async XLA Ops:
  0.6 2.3 %copy-start.1 = (s32[1,1,4,3]{2,1,3,0:T(1,128)S(1)}, s32[1,1,4,3]{2,1,3,0:T(1,128)}, u32[]{:S(2)}) copy-start(s32[1,1,4,3]{2,1,3,0:T(1,128)} %param.14) | copy-start | bytes 148
  0.6 3.0 %copy-start = (bf16[1,1,4,3,3,3,3]{6,2,5,4,3,1,0:T(4,128)(2,1)S(1)}, bf16[1,1,4,3,3,3,3]{6,2,5,4,3,1,0:T(4,128)(2,1)}, u32[]{:S(2)}) copy-start(bf16[1,1,4,3,3,3,3]{6,2,5,4,3,1,0:T(4,128)(2,1)} %param.12) | copy-start | bytes 1948
  12.3 9.5 %copy-start.2 = (bf16[1152,128]{1,0:T(8,128)(2,1)S(1)}, bf16[1152,128]{1,0:T(8,128)(2,1)}, u32[]{:S(2)}) copy-start(bf16[1152,128]{1,0:T(8,128)(2,1)} %get-tuple-element.32) | copy-start | bytes 884740
  19.7 19.3 %collective-permute-start = (bf16[1152,128]{1,0:T(8,128)(2,1)}, bf16[1152,128]{1,0:T(8,128)(2,1)S(1)}, u32[]{:S(2)}, u32[]{:S(2)}) collective-permute-start(bf16[1152,128]{1,0:T(8,128)(2,1)} %get-tuple-element.30), channel_id=1, source_target_pairs={{1,0},{2,1},{3,2},{4,3},{5,4},{6,5},{7,6},{8,7},{9,8},{10,9},{11,1... | collective-permute-start | bytes 884744 | tf_op jit(solution)/shard_map/ppermute | solution.py:347
  21.7 17.2 %collective-permute-start.1 = (bf16[1152,128]{1,0:T(8,128)(2,1)S(1)}, bf16[1152,128]{1,0:T(8,128)(2,1)S(1)}, u32[]{:S(2)}, u32[]{:S(2)}) collective-permute-start(bf16[1152,128]{1,0:T(8,128)(2,1)S(1)} %copy-done.2), channel_id=1, source_target_pairs={{16,0},{32,16},{48,32},{64,48},{80,64},{96,80},{112,96},{128,112},... | collective-permute-start | bytes 884744 | tf_op jit(solution)/shard_map/ppermute | solution.py:347
  39.0 0.7 copy-start.5
  39.0 0.8 copy-start.6
  57.3 11.6 %collective-permute-start.2 = (bf16[1152,128]{1,0:T(8,128)(2,1)}, bf16[1152,128]{1,0:T(8,128)(2,1)S(1)}, u32[]{:S(2)}, u32[]{:S(2)}) collective-permute-start(bf16[1152,128]{1,0:T(8,128)(2,1)} %get-tuple-element.33.left), channel_id=1, source_target_pairs={{15,0},{0,1},{1,2},{2,3},{3,4},{4,5},{5,6},{6,7},{7,8},{8,9},{9,10... | collective-permute-start | bytes 884744 | tf_op jit(solution)/shard_map/ppermute | solution.py:347
  57.3 14.7 %collective-permute-start.3 = (bf16[1152,128]{1,0:T(8,128)(2,1)}, bf16[1152,128]{1,0:T(8,128)(2,1)S(1)}, u32[]{:S(2)}, u32[]{:S(2)}) collective-permute-start(bf16[1152,128]{1,0:T(8,128)(2,1)} %get-tuple-element.34.top), channel_id=1, source_target_pairs={{240,0},{0,16},{16,32},{32,48},{48,64},{64,80},{80,96},{96,112},{1... | collective-permute-start | bytes 884744 | tf_op jit(solution)/shard_map/ppermute | solution.py:347
  68.9 3.0 %copy-start.3 = (bf16[1152,128]{1,0:T(8,128)(2,1)}, bf16[1152,128]{1,0:T(8,128)(2,1)S(1)}, u32[]{:S(2)}) copy-start(bf16[1152,128]{1,0:T(8,128)(2,1)S(1)} %collective-permute-done.2.above) | copy-start | bytes 884740
  72.0 0.7 copy-start.4
where the time goes:
time: 86.9 us; the launch traced here: 86.6 us
  Pallas kernels  56.2 us (65%)
  waiting for transfers between devices  14.7 us (17%)
  starting transfers between devices  9.97 us (11%)
  local copies, waits for them, and re-layouts  5.13 us (6%)
    pallas_call x5, Pallas kernels, call(): pl.pallas_call(body, name=name, out_shape=tuple(outs), in_specs=smem_in(l...  56.2 us
    ppermute x4, waiting for transfers between devices, from_behind(): return lax.ppermute(block, axis, route)  14.7 us
    ppermute x4, starting transfers between devices, from_behind(): return lax.ppermute(block, axis, route)  9.97 us
    squeeze x1, local copies, waits for them, and re-layouts, shards(): sketches = [sketch[0, 0, i] for i in range(4)]  2.28 us
    unnamed x16, local copies, waits for them, and re-layouts  2.18 us
  transfers between devices with their start and end apart: 4, of which 2 were waited for; matrix products, arithmetic and copies ran while one was open for 0% of the time, Pallas kernels for 11%

commit v1 on v0

v1 whole, which is shorter than its diff:
```python
import functools

import jax
import jax.numpy as jnp
from jax import lax
from jax.experimental import pallas as pl
from jax.experimental.pallas import tpu as pltpu
from jax.sharding import PartitionSpec as P

F32 = jnp.float32
BF16 = jnp.bfloat16
CHI = 128
D2 = 9
CUT = CHI * D2
TALL = CHI * 8
LAY = 96
GROUP = 32
CHUNKS = CHI // GROUP
ROWS = GROUP * 8
VMEM = 24 * 1024 * 1024


def dot(a, b):
    return lax.dot_general(a, b, (((1,), (0,)), ((), ())), preferred_element_type=F32)


def dot_nt(a, b):
    return lax.dot_general(a, b, (((1,), (1,)), ((), ())), preferred_element_type=F32)


def dot_tn(a, b):
    return lax.dot_general(a, b, (((0,), (0,)), ((), ())), preferred_element_type=F32)


def exact_tn(a, b):
    return lax.dot_general(
        a, b, (((0,), (0,)), ((), ())), precision=lax.Precision.HIGHEST, preferred_element_type=F32
    )


def exact_nt(a, b):
    return lax.dot_general(
        a, b, (((1,), (1,)), ((), ())), precision=lax.Precision.HIGHEST, preferred_element_type=F32
    )


def slab(ref, p):
    return ref[p * CHI : (p + 1) * CHI, :]


def side_by_side(ref):
    return jnp.concatenate([slab(ref, p) for p in range(D2)], axis=1)


def pack_rows(slab_of, wide, out):
    for p in range(8):
        wide[pl.ds(p, CHI, stride=8), :] = slab_of(p).astype(F32)
    out[0:TALL, :] = wide[0:TALL, :].astype(BF16)
    out[TALL:CUT, :] = slab_of(8).astype(BF16)


def packed_slab(wide, p):
    return wide[pl.ds(p, CHI, stride=8), :] if p < 8 else wide[TALL:CUT, :]


def chain(left, right, layer, thin, consume):
    thin[...] = jnp.zeros_like(thin)
    last = dot(left[TALL:CUT, :], right[...])
    for q in range(D2):
        thin[pl.ds(q, CHI, stride=16), :] = last[:, q * CHI : (q + 1) * CHI]
    blank = jnp.zeros((8, CHI), F32)
    for chunk in range(CHUNKS):
        rows = slice(chunk * ROWS, (chunk + 1) * ROWS)
        three = dot(left[rows, :], right[...])
        stacks = []
        for f in range(GROUP):
            here = (chunk * GROUP + f) * 16
            parts = [three[f * 8 : f * 8 + 8, q * CHI : (q + 1) * CHI] for q in range(D2)]
            stack = jnp.concatenate(parts + [thin[here : here + 16, :], blank], axis=0)
            stacks.append(stack.astype(BF16))
        mixed = dot(layer[...], jnp.concatenate(stacks, axis=1))
        tall = []
        for f in range(GROUP):
            here = (chunk * GROUP + f) * 16
            lanes = slice(f * CHI, (f + 1) * CHI)
            thin[here : here + 16, :] = mixed[72:88, lanes]
            tall.append(
                jnp.concatenate([mixed[s * 8 : s * 8 + 8, lanes] for s in range(D2)], axis=1)
            )
        consume(rows, jnp.concatenate(tall, axis=0).astype(BF16))
    rest = [thin[pl.ds(s, CHI, stride=16), :].astype(BF16) for s in range(D2)]
    consume(slice(TALL, CUT), jnp.concatenate(rest, axis=1))


def third(n):
    return (n * 11) >> 5


def layer_masks():
    row = lax.broadcasted_iota(jnp.int32, (LAY, 81), 0)
    lane = lax.broadcasted_iota(jnp.int32, (LAY, 81), 1)
    late = row >= 72
    slow = jnp.where(late, row - 72, row >> 3)
    fast = jnp.where(late, 8, row & 7)
    valid = row < 81
    pairs = ((third(slow), third(fast)), (slow - 3 * third(slow), fast - 3 * third(fast)))
    leg_l = (lane * 19) >> 9
    rest = lane - 27 * leg_l
    leg_u = (rest * 57) >> 9
    rest = rest - 9 * leg_u
    leg_r = (rest * 11) >> 5
    leg_d = rest - 3 * leg_r

    def mask(slow_leg, fast_leg):
        return [
            jnp.where(valid & (slow_leg == a) & (fast_leg == b), 1.0, 0.0).astype(F32)
            for a, b in pairs
        ]

    return mask(leg_r, leg_u), mask(leg_d, leg_l), mask(leg_r, leg_d), mask(leg_u, leg_l)


def kept_rows(site, phys, virt):
    lane = lax.broadcasted_iota(jnp.int32, (4, 81), 1)
    state = lax.broadcasted_iota(jnp.int32, (4, 81), 0)
    leg_l = (lane * 19) >> 9
    rest = lane - 27 * leg_l
    leg_u = (rest * 57) >> 9
    rest = rest - 9 * leg_u
    leg_r = (rest * 11) >> 5
    leg_d = rest - 3 * leg_r
    total = jnp.zeros((4, 81), jnp.int32)
    for s in range(4):
        total = total + jnp.where(state == s, phys[s], 0)
    for i in range(3):
        total = total + jnp.where(leg_l == i, virt[i, 0, 0], 0)
        total = total + jnp.where(leg_u == i, virt[i, 0, 1], 0)
        total = total - jnp.where(leg_r == i, virt[i, 0, 2], 0)
        total = total - jnp.where(leg_d == i, virt[i, 0, 3], 0)
    return jnp.where(total == 0, site[...].astype(F32), 0.0)


def build_layers(kept, out_a, out_b, out_c):
    m_ru, m_dl, m_rd, m_ul = layer_masks()

    def build(rows, cols):
        halves = []
        for half in range(2):
            tall = jnp.concatenate([rows[half] * kept[s : s + 1, :] for s in range(4)], axis=0)
            halves.append(dot_nt(tall.astype(BF16), cols[half].astype(BF16)))
        ket_bra = halves[0] * halves[1]
        total = ket_bra[:LAY]
        for s in range(1, 4):
            total = total + ket_bra[s * LAY : (s + 1) * LAY]
        return total.astype(BF16)

    out_a[...] = build(m_dl, m_ru)
    out_b[...] = build(m_ru, m_dl)
    out_c[...] = build(m_rd, m_ul)


def unpack_term(wide, term):
    for p in range(D2):
        term[p * CHI : (p + 1) * CHI, :] = packed_slab(wide, p).astype(term.dtype)


def right_kernel(
    phys, virt, site, corner, edge_r, edge_t, sketches,
    term, lay_a, lay_b, lay_c, pair_out, rows_t,
    wide, thin, sketch, arrived,
):
    coming = fetch(sketches, 3, sketch, arrived)
    build_layers(kept_rows(site, phys, virt), lay_a, lay_b, lay_c)
    pair_out[...] = dot(corner[...], side_by_side(edge_r)).astype(BF16)
    pack_rows(lambda p: slab(edge_t, p), wide, rows_t)
    coming.wait()

    def consume(rows, block):
        wide[rows, :] = dot(block, sketch[...])

    chain(rows_t, pair_out, lay_a, thin, consume)
    unpack_term(wide, term)


def lower_kernel(
    corner, edge_b, edge_l, lay_b, sketches,
    term, pair_out, rows_l,
    wide, thin, sketch, arrived,
):
    coming = fetch(sketches, 1, sketch, arrived)
    pair_out[...] = dot(corner[...], side_by_side(edge_b)).astype(BF16)
    pack_rows(lambda p: slab(edge_l, p), wide, rows_l)
    coming.wait()

    def consume(rows, block):
        wide[rows, :] = dot(block, sketch[...])

    chain(rows_l, pair_out, lay_b, thin, consume)
    unpack_term(wide, term)


def upper_kernel(
    corner, edge_t, edge_l, lay_c, sketches,
    own_left, own_top, corner_edge, corner_side,
    left_rows, sketch_cols, sketch_rows, wide, thin, top_sum,
    sketch_l, sketch_t, arrived_l, arrived_t,
):
    coming_l = fetch(sketches, 0, sketch_l, arrived_l)
    coming_t = fetch(sketches, 2, sketch_t, arrived_t)
    corner_edge[...] = dot(corner[...], side_by_side(edge_t)).astype(BF16)
    corner_side[...] = dot_tn(corner[...], side_by_side(edge_l)).astype(BF16)
    pack_rows(lambda p: jnp.transpose(slab(edge_l, p).astype(F32)), wide, left_rows)
    coming_l.wait()
    wide[...] = sketch_l[...].astype(F32)
    for p in range(D2):
        sketch_cols[p * CHI : (p + 1) * CHI, :] = wide[pl.ds(p, CHI, stride=D2), :].astype(BF16)
    coming_t.wait()
    wide[...] = sketch_t[...].astype(F32)
    picked = [wide[pl.ds(p, CHI, stride=D2), :] for p in range(D2)]
    pack_rows(lambda p: picked[p], wide, sketch_rows)
    top_sum[...] = jnp.zeros_like(top_sum)

    def consume(rows, block):
        wide[rows, :] = dot(block, sketch_cols[...])
        top_sum[...] += dot_tn(sketch_rows[rows, :], block)

    chain(left_rows, corner_edge, lay_c, thin, consume)
    unpack_term(wide, own_left)
    for p in range(D2):
        own_top[p * CHI : (p + 1) * CHI, :] = jnp.transpose(top_sum[:, p * CHI : (p + 1) * CHI])


BLOCK = 32


def reciprocal(x):
    r = pl.reciprocal(x, approx=True)
    r = r * (2.0 - x * r)
    return r * (2.0 - x * r)


def spread(rows, p):
    return jnp.broadcast_to(rows[p : p + 1, :], (8, CHI))


def eliminate(grams):
    count = len(grams)
    sub = lax.broadcasted_iota(jnp.int32, (8, CHI), 0)
    lane = lax.broadcasted_iota(jnp.int32, (8, CHI), 1)
    groups = CHI // 8
    fact = [[g[8 * i : 8 * i + 8, :] for i in range(groups)] for g in grams]
    inv = [
        [jnp.where(lane == sub + 8 * i, 1.0, 0.0).astype(F32) for i in range(groups)] for _ in grams
    ]
    for start in range(0, groups, BLOCK // 8):
        end = start + BLOCK // 8
        for b in range(start, end):
            cols = [
                [
                    [
                        jnp.broadcast_to(fact[m][g][:, 8 * b + j : 8 * b + j + 1], (8, CHI))
                        for j in range(8)
                    ]
                    for g in range(b, end)
                ]
                for m in range(count)
            ]
            pivots = [jnp.zeros((8, CHI), F32) for _ in grams]
            for p in range(0, 8, 2):
                q = p + 1
                for m in range(count):
                    head = cols[m][0]
                    one, off, two = spread(head[p], p), spread(head[q], p), spread(head[q], q)
                    det = one * two - off * off
                    over_one, over_det = reciprocal(one), reciprocal(det)
                    lead = off * over_one
                    pivots[m] = jnp.where(
                        sub == p, one, jnp.where(sub == q, det * over_one, pivots[m])
                    )
                    later = range(q + 1, 8)
                    row_p = [spread(head[j], p) for j in later]
                    row_q = [spread(head[j], q) for j in later]
                    fact_p, fact_q = spread(fact[m][b], p), spread(fact[m][b], q)
                    inv_p, inv_q = spread(inv[m][b], p), spread(inv[m][b], q)
                    one_d, off_d, two_d = one * over_det, off * over_det, two * over_det
                    for g in range(b, end):
                        own = cols[m][g - b]
                        by_p = own[p] * two_d - own[q] * off_d
                        by_q = own[q] * one_d - own[p] * off_d
                        if g == b:
                            by_p = jnp.where(sub > q, by_p, jnp.where(sub == q, lead, 0.0))
                            by_q = jnp.where(sub > q, by_q, 0.0)
                        for n, j in enumerate(later):
                            own[j] = own[j] - by_p * row_p[n] - by_q * row_q[n]
                        fact[m][g] = fact[m][g] - by_p * fact_p - by_q * fact_q
                        inv[m][g] = inv[m][g] - by_p * inv_p - by_q * inv_q
            for m in range(count):
                root = lax.rsqrt(pivots[m])
                fact[m][b] = fact[m][b] * root
                inv[m][b] = inv[m][b] * root
        if end < groups:
            for m in range(count):
                upper = jnp.concatenate(fact[m][start:end], axis=0)
                both = jnp.concatenate([upper, jnp.concatenate(inv[m][start:end], axis=0)], axis=1)
                update = exact_tn(upper, both)
                for g in range(end, groups):
                    fact[m][g] = fact[m][g] - update[8 * g : 8 * g + 8, :CHI]
                    inv[m][g] = inv[m][g] - update[8 * g : 8 * g + 8, CHI:]
    return [jnp.concatenate(i, axis=0) for i in inv]


def basis_kernel(virt, env, own_left, below, own_top, beside, left_out, top_out, range_l, range_t):
    row = lax.broadcasted_iota(jnp.int32, (CHI, CHI), 0)
    col = lax.broadcasted_iota(jnp.int32, (CHI, CHI), 1)
    grams = []
    for side, (own, other, ranged, leg) in enumerate(
        ((own_left, below, range_l, 3), (own_top, beside, range_t, 2))
    ):
        across = jnp.broadcast_to(env[side : side + 1, :].astype(F32), (CHI, CHI))
        gap = across - jnp.transpose(across)
        for p in range(D2):
            shift = (virt[p // 3, 0, leg] - virt[p % 3, 0, leg]).astype(F32)
            total = slab(own, p) + slab(other, p).astype(F32)
            ranged[p * CHI : (p + 1) * CHI, :] = jnp.where(gap == shift, total, 0.0)
        gram = exact_tn(ranged[...], ranged[...])
        diagonal = jnp.where(row == col, gram, 0.0)
        mean = jnp.sum(jnp.sum(diagonal, axis=1, keepdims=True), axis=0, keepdims=True) / CHI
        grams.append(gram + jnp.where(row == col, 0.01 * mean + 1e-06, 0.0))
    inverses = eliminate(grams)
    left_out[...] = exact_nt(range_l[...], inverses[0]).astype(BF16)
    top_out[...] = exact_nt(range_t[...], inverses[1]).astype(BF16)


def unit(values):
    square = jnp.sum(jnp.sum(values * values, axis=1, keepdims=True), axis=0, keepdims=True)
    return (values / jnp.sqrt(square / values.size + 1e-06)).astype(BF16)


def slab_rows(wide_ref, p):
    return wide_ref[:, p * CHI : (p + 1) * CHI]


def corner_from(projector, pair):
    tall = jnp.concatenate([slab_rows(pair, p) for p in range(D2)], axis=0)
    return dot_tn(projector[...], tall)


def own_kernel(
    left, top, rows_l, rows_t, lay_a, lay_b, lower_pair, right_pair,
    out_ll, out_tr, mixed_l, mixed_t,
    beside, thin,
):
    for own, natural, layer, mixed in ((left, rows_l, lay_b, mixed_l), (top, rows_t, lay_a, mixed_t)):
        beside[...] = side_by_side(own)

        def consume(rows, block):
            mixed[rows, :] = block

        chain(natural, beside, layer, thin, consume)
    out_ll[...] = unit(corner_from(left, lower_pair))
    out_tr[...] = unit(corner_from(top, right_pair))


def final_kernel(
    above, before, mixed_l, mixed_t, corner_edge, corner_side,
    out_lu, out_le, out_tl, out_te,
    packed, wide,
):
    for other, mixed, out in ((above, mixed_l, out_le), (before, mixed_t, out_te)):
        pack_rows(lambda p: slab(other, p), wide, packed)
        result = unit(dot_tn(packed[...], mixed[...]))
        for p in range(D2):
            out[p * CHI : (p + 1) * CHI, :] = result[:, p * CHI : (p + 1) * CHI]
    out_lu[...] = unit(corner_from(above, corner_edge))
    out_tl[...] = unit(jnp.transpose(corner_from(before, corner_side)))


def shape(*dims, dtype=BF16):
    return jax.ShapeDtypeStruct(dims, dtype)


def vmem_in(count):
    return [pl.BlockSpec(memory_space=pltpu.VMEM)] * count


def smem_in(count):
    return [pl.BlockSpec(memory_space=pltpu.SMEM)] * count


def fetch(sketches, index, buffer, arrived):
    copy = pltpu.make_async_copy(sketches.at[pl.ds(index * CUT, CUT), :], buffer, arrived)
    copy.start()
    return copy


def call(body, name, smem, ins, outs, scratch, flops, fetches=0):
    moved = sum(a.size * a.dtype.itemsize for a in ins) + sum(
        o.size * jnp.dtype(o.dtype).itemsize for o in outs
    )
    specs = vmem_in(len(ins))
    buffers = [pltpu.VMEM(s, d) for s, d in scratch]
    if fetches:
        specs[-1] = pl.BlockSpec(memory_space=pl.ANY)
        buffers += [pltpu.VMEM((CUT, CHI), BF16)] * fetches + [pltpu.SemaphoreType.DMA] * fetches
    return pl.pallas_call(
        body,
        name=name,
        out_shape=tuple(outs),
        in_specs=smem_in(len(smem)) + specs,
        out_specs=tuple(vmem_in(len(outs))),
        scratch_shapes=buffers,
        compiler_params=pltpu.CompilerParams(vmem_limit_bytes=VMEM),
        cost_estimate=pl.CostEstimate(flops=flops, bytes_accessed=moved, transcendentals=0),
    )(*smem, *ins)


def from_behind(block, axis, distance):
    size = lax.axis_size(axis)
    route = [((i - distance) % size, i) for i in range(size)]
    return lax.ppermute(block, axis, route)


SEND = BF16


def flat(edge):
    return edge.transpose(1, 0, 2).reshape(CUT, CHI)


def shards(
    site_tensor, phys_charge, virt_charge, env_charge, corner_ul, corner_ur, corner_ll,
    edge_top, edge_right, edge_bottom, edge_left, sketch,
):
    site = site_tensor[0, 0].reshape(4, 81)
    phys, env = phys_charge[0, 0], env_charge[0, 0]
    virt = virt_charge[0, 0].T[:, None, :]
    ul, ur, ll = corner_ul[0, 0], corner_ur[0, 0], corner_ll[0, 0]
    top, right, bottom, left = (
        flat(e[0, 0]) for e in (edge_top, edge_right, edge_bottom, edge_left)
    )
    sketches = sketch[0, 0].reshape(4 * CUT, CHI)
    tall = shape(CUT, CHI)
    broad = shape(CHI, CUT)
    lay = shape(LAY, LAY)
    wide = ((CUT, CHI), F32)
    thin = ((CHI * 16, CHI), F32)
    square = shape(CUT, CUT)
    work = 1_000_000_000
    from_right, lay_a, lay_b, lay_c, right_pair, rows_t = call(
        right_kernel, "right", [phys, virt], [site, ur, right, top, sketches],
        [shape(CUT, CHI, dtype=SEND), lay, lay, lay, broad, tall], [wide, thin], work, 1,
    )
    beside = from_behind(from_right, "lx", -1)
    from_lower, lower_pair, rows_l = call(
        lower_kernel, "lower", [], [ll, bottom, left, lay_b, sketches],
        [shape(CUT, CHI, dtype=SEND), broad, tall], [wide, thin], work, 1,
    )
    below = from_behind(from_lower, "ly", -1)
    own_left, own_top, corner_edge, corner_side = call(
        upper_kernel, "upper", [], [ul, top, left, lay_c, sketches],
        [shape(CUT, CHI, dtype=F32), shape(CUT, CHI, dtype=F32), broad, broad],
        [((CUT, CHI), BF16), ((CUT, CHI), BF16), ((CUT, CHI), BF16), wide, thin, ((CHI, CUT), F32)],
        work, 2,
    )
    left_basis, top_basis = call(
        basis_kernel, "basis", [virt], [env, own_left, below, own_top, beside], [tall, tall],
        [((CUT, CHI), F32), ((CUT, CHI), F32)], work,
    )
    before = from_behind(top_basis, "lx", 1)
    above = from_behind(left_basis, "ly", 1)
    corner = shape(CHI, CHI)
    lo, tr, mixed_l, mixed_t = call(
        own_kernel, "own", [],
        [left_basis, top_basis, rows_l, rows_t, lay_a, lay_b, lower_pair, right_pair],
        [corner, corner, square, square], [((CHI, CUT), BF16), thin], work,
    )
    lu, le, tl, te = call(
        final_kernel, "final", [], [above, before, mixed_l, mixed_t, corner_edge, corner_side],
        [corner, tall, corner, tall], [((CUT, CHI), BF16), wide], work,
    )
    lift = lambda a: a[None, None]
    edge = lambda a: a.reshape(D2, CHI, CHI).transpose(1, 0, 2)[None, None]
    return lift(lu), edge(le), lift(lo), lift(tl), edge(te), lift(tr)


def solution(mesh):
    split = lambda rest: P("lx", "ly", *([None] * rest))
    in_specs = tuple(split(rest) for rest in (5, 1, 2, 2, 2, 2, 2, 3, 3, 3, 3, 3))
    out_specs = tuple(split(rest) for rest in (2, 3, 2, 2, 3, 2))
    return jax.shard_map(shards, mesh=mesh, in_specs=in_specs, out_specs=out_specs, check_vma=False)
```

time: 86.9 us -> 57.5 us (0.66)
  the two profiles are of different devices: /device:TPU:8 before, /device:TPU:1 now
where the time goes in v1:
time: 57.5 us; the launch traced here: 57.1 us
  Pallas kernels  28.6 us (50%)
  starting transfers between devices  13.6 us (24%)
  waiting for transfers between devices  7.98 us (14%)
  local copies, waits for them, and re-layouts  6.19 us (11%)
  between operations  0.76 us (1%)
    pallas_call x6, Pallas kernels, call(): pl.pallas_call(body, name=name, out_shape=tuple(outs), in_specs=smem_in(l...  28.6 us
    ppermute x4, starting transfers between devices, from_behind(): return lax.ppermute(block, axis, route)  13.6 us
    ppermute x4, waiting for transfers between devices, from_behind(): return lax.ppermute(block, axis, route)  7.98 us
    unnamed x23, local copies, waits for them, and re-layouts  5.39 us
  transfers between devices with their start and end apart: 4, of which 1 were waited for; matrix products, arithmetic and copies ran while one was open for 0% of the time, Pallas kernels for 17%

profile of v1, /device:TPU:1, one launch (start us, length us, event | category | flops | bytes accessed | tf_op | source)
XLA Modules:
  0.0 57.1 jit_solution(11229662077021004221)
XLA Ops:
  0.6 0.7 %copy.30 = s32[1,1,4,3]{2,3,0,1:T(4,128)S(1)} copy(s32[1,1,4,3]{2,1,3,0:T(1,128)} %param.14) | data formatting | bytes 96 | tf_op jit(solution)/shard_map/transpose | solution.py:436
  1.3 0.8 %copy.25 = bf16[1,1,4,3,3,3,3]{6,5,4,3,2,1,0:T(4,128)(2,1)S(1)} copy(bf16[1,1,4,3,3,3,3]{6,2,5,4,3,1,0:T(4,128)(2,1)} %param.12) | data formatting | bytes 1296 | tf_op args[0]
  2.1 0.1 reshape_squeeze.6.site
  2.2 0.0 copy-start
  2.2 1.3 %copy-done = bf16[1,1,4,1152,128]{4,3,2,1,0:T(8,128)(2,1)S(1)} copy-done((bf16[1,1,4,1152,128]{4,3,2,1,0:T(8,128)(2,1)S(1)}, bf16[1,1,4,1152,128]{4,3,2,1,0:T(8,128)(2,1)}, u32[]{:S(2)}) %copy-start) | copy-done | bytes 1179672
  3.5 1.0 %copy-done.2 = bf16[1,1,128,9,128]{4,2,3,1,0:T(8,128)(2,1)S(1)} copy-done((bf16[1,1,128,9,128]{4,2,3,1,0:T(8,128)(2,1)S(1)}, bf16[1,1,128,9,128]{4,2,3,1,0:T(8,128)(2,1)}, u32[]{:S(2)}) %copy-start.2) | copy-done | bytes 294936
  4.4 1.0 %copy-done.4 = bf16[1,1,128,9,128]{4,2,3,1,0:T(8,128)(2,1)S(1)} copy-done((bf16[1,1,128,9,128]{4,2,3,1,0:T(8,128)(2,1)S(1)}, bf16[1,1,128,9,128]{4,2,3,1,0:T(8,128)(2,1)}, u32[]{:S(2)}) %copy-start.4) | copy-done | bytes 294936
  5.4 0.8 %copy-done.6 = bf16[1,1,128,128]{3,2,1,0:T(8,128)(2,1)S(1)} copy-done((bf16[1,1,128,128]{3,2,1,0:T(8,128)(2,1)S(1)}, bf16[1,1,128,128]{3,2,1,0:T(8,128)(2,1)}, u32[]{:S(2)}) %copy-start.6) | copy-done | bytes 32792
  6.2 0.7 %copy-done.10 = s32[1,1,4]{2,1,0:T(1,128)S(1)} copy-done((s32[1,1,4]{2,1,0:T(1,128)S(1)}, s32[1,1,4]{2,1,0:T(1,128)}, u32[]{:S(2)}) %copy-start.10) | copy-done | bytes 40
  6.8 4.4 %right.1 = (bf16[1152,128]{1,0:T(8,128)(2,1)S(1)}, bf16[96,96]{1,0:T(8,128)(2,1)S(1)}, bf16[96,96]{1,0:T(8,128)(2,1)S(1)}, bf16[96,96]{1,0:T(8,128)(2,1)S(1)}, b...) custom-call(s32[4]{0:T(128)S(1)} %bitcast.60, s32[3,1,4]{2,1,0:T(1,128)S(1)} %copy.27.virt, ...), custom_call_target="tpu_custom_call" | custom-call | flops 1000000000 | bytes 2742920 | tf_op jit(solution)/shard_map/right/pallas_call | solution.py:405
  11.2 0.0 copy-start.8
  11.3 3.6 %lower.1 = (bf16[1152,128]{1,0:T(8,128)(2,1)S(1)}, bf16[128,1152]{1,0:T(8,128)(2,1)S(1)}, bf16[1152,128]{1,0:T(8,128)(2,1)S(1)}) custom-call(bf16[128,128]{1,0:T(8,128)(2,1)S(1)} %bitcast.57, bf16[1152,128]{1,0:T(8,128)(2,1)S(1)} %bitcast.51, bf16[1152,128]{1,0:T(8,128)(2,1)S(1)} %bitcast.54, bf16[96,96]{1,0:T(8,128)(2,1)S(1)} %get-tuple-element.31.lay_b, ...), custom_call_target="tpu_custom_call" | custom-call | flops 1000000000 | bytes 2705408 | tf_op jit(solution)/shard_map/lower/pallas_call | solution.py:405
  15.0 0.0 copy-start.9
  15.0 3.3 %collective-permute-start = (bf16[1152,128]{1,0:T(8,128)(2,1)S(1)}, bf16[1152,128]{1,0:T(8,128)(2,1)S(1)}, u32[]{:S(2)}, u32[]{:S(2)}) collective-permute-start(bf16[1152,128]{1,0:T(8,128)(2,1)S(1)} %get-tuple-element.32), channel_id=1, source_target_pairs={{1,0},{2,1},{3,2},{4,3},{5,4},{6,5},{7,6},{8,7},{9,8},{10,9},{11,1... | collective-permute-start | bytes 884744 | tf_op jit(solution)/shard_map/ppermute | solution.py:420
  18.3 6.5 %collective-permute-start.1 = (bf16[1152,128]{1,0:T(8,128)(2,1)S(1)}, bf16[1152,128]{1,0:T(8,128)(2,1)S(1)}, u32[]{:S(2)}, u32[]{:S(2)}) collective-permute-start(bf16[1152,128]{1,0:T(8,128)(2,1)S(1)} %get-tuple-element.34), channel_id=1, source_target_pairs={{16,0},{32,16},{48,32},{64,48},{80,64},{96,80},{112,96},{128,112},... | collective-permute-start | bytes 884744 | tf_op jit(solution)/shard_map/ppermute | solution.py:420
  24.7 4.5 %upper.1 = (f32[1152,128]{1,0:T(8,128)S(1)}, f32[1152,128]{1,0:T(8,128)S(1)}, bf16[128,1152]{1,0:T(8,128)(2,1)S(1)}, bf16[128,1152]{1,0:T(8,128)(2,1)S(1)}) custom-call(bf16[128,128]{1,0:T(8,128)(2,1)S(1)} %bitcast.58, bf16[1152,128]{1,0:T(8,128)(2,1)S(1)} %bitcast.53, bf16[1152,128]{1,0:T(8,128)(2,1)S(1)} %bitcast.55, ...), custom_call_target="tpu_custom_call" | custom-call | flops 1000000000 | bytes 3590144 | tf_op jit(solution)/shard_map/upper/pallas_call | solution.py:405
  29.3 0.0 collective-permute-done.below
  29.3 0.0 collective-permute-done.1.beside
  29.3 8.3 %basis.1 = (bf16[1152,128]{1,0:T(8,128)(2,1)S(1)}, bf16[1152,128]{1,0:T(8,128)(2,1)S(1)}) custom-call(s32[3,1,4]{2,1,0:T(1,128)S(1)} %copy.27.virt, s32[2,128]{1,0:T(2,128)S(1)} %bitcast.59, f32[1152,128]{1,0:T(8,128)S(1)} %get-tuple-element.30.own_left, bf16[1152,128]{1,0:T(8,128)(2,1)S(1)} %collective-permute-done.below, ...), custom_call_target="tpu_custom_call" | custom-call | flops 1000000000 | bytes 2360320 | tf_op jit(solution)/shard_map/basis/pallas_call | solution.py:405
  37.6 3.8 %collective-permute-start.2 = (bf16[1152,128]{1,0:T(8,128)(2,1)S(1)}, bf16[1152,128]{1,0:T(8,128)(2,1)S(1)}, u32[]{:S(2)}, u32[]{:S(2)}) collective-permute-start(bf16[1152,128]{1,0:T(8,128)(2,1)S(1)} %get-tuple-element.35.left), channel_id=1, source_target_pairs={{15,0},{0,1},{1,2},{2,3},{3,4},{4,5},{5,6},{6,7},{7,8},{8,9},{9,10... | collective-permute-start | bytes 884744 | tf_op jit(solution)/shard_map/ppermute | solution.py:420
  41.4 0.0 collective-permute-start.3
  41.4 5.3 %own.1 = (bf16[128,128]{1,0:T(8,128)(2,1)}, bf16[128,128]{1,0:T(8,128)(2,1)}, bf16[1152,1152]{1,0:T(8,128)(2,1)S(1)}, bf16[1152,1152]{1,0:T(8,128)(2,1)S(1)}) custom-call(bf16[1152,128]{1,0:T(8,128)(2,1)S(1)} %get-tuple-element.35.left, bf16[1152,128]{1,0:T(8,128)(2,1)S(1)} %get-tuple-element.36.top, bf16[1152,128]{1,0:T(8,128)(2,1)S(1)} %get-tuple-element.37.rows_l, ...), custom_call_target="tpu_custom_call" | custom-call | flops 1000000000 | bytes 7180288 | tf_op jit(solution)/shard_map/own/pallas_call | solution.py:405
  46.7 8.0 %collective-permute-done.3.before = bf16[1152,128]{1,0:T(8,128)(2,1)S(1)} collective-permute-done((bf16[1152,128]{1,0:T(8,128)(2,1)S(1)}, bf16[1152,128]{1,0:T(8,128)(2,1)S(1)}, u32[]{:S(2)}, u32[]{:S(2)}) %collective-permute-start.3) | collective-permute-done | bytes 294944 | tf_op jit(solution)/shard_map/ppermute | solution.py:420
  54.7 2.4 %final.1 = (bf16[128,128]{1,0:T(8,128)(2,1)}, bf16[1152,128]{1,0:T(8,128)(2,1)}, bf16[128,128]{1,0:T(8,128)(2,1)}, bf16[1152,128]{1,0:T(8,128)(2,1)}) custom-call(bf16[1152,128]{1,0:T(8,128)(2,1)S(1)} %collective-permute-done.2.above, bf16[1152,128]{1,0:T(8,128)(2,1)S(1)} %collective-permute-done.3.before, bf16[1152,1152]{1,0:T(8,128)(2,1)S(1)} %get-tuple-element.42.mixed_l, ...), custom_call_target="tpu_custom_call" | custom-call | flops 1000000000 | bytes 7143424 | tf_op jit(solution)/shard_map/final/pallas_call | solution.py:405
  (16 shorter events, 0.0 us)
Async XLA Ops:
  0.6 10.6 %copy-start.7 = (bf16[1,1,128,128]{3,2,1,0:T(8,128)(2,1)S(1)}, bf16[1,1,128,128]{3,2,1,0:T(8,128)(2,1)}, u32[]{:S(2)}) copy-start(bf16[1,1,128,128]{3,2,1,0:T(8,128)(2,1)} %param.18) | copy-start | bytes 98308
  2.2 1.3 %copy-start = (bf16[1,1,4,1152,128]{4,3,2,1,0:T(8,128)(2,1)S(1)}, bf16[1,1,4,1152,128]{4,3,2,1,0:T(8,128)(2,1)}, u32[]{:S(2)}) copy-start(bf16[1,1,4,1152,128]{4,3,2,1,0:T(8,128)(2,1)} %param.23) | copy-start | bytes 3538948
  3.5 1.0 %copy-start.2 = (bf16[1,1,128,9,128]{4,2,3,1,0:T(8,128)(2,1)S(1)}, bf16[1,1,128,9,128]{4,2,3,1,0:T(8,128)(2,1)}, u32[]{:S(2)}) copy-start(bf16[1,1,128,9,128]{4,2,3,1,0:T(8,128)(2,1)} %param.20) | copy-start | bytes 884740
  4.4 1.0 %copy-start.4 = (bf16[1,1,128,9,128]{4,2,3,1,0:T(8,128)(2,1)S(1)}, bf16[1,1,128,9,128]{4,2,3,1,0:T(8,128)(2,1)}, u32[]{:S(2)}) copy-start(bf16[1,1,128,9,128]{4,2,3,1,0:T(8,128)(2,1)} %param.19) | copy-start | bytes 884740
  5.4 0.8 %copy-start.6 = (bf16[1,1,128,128]{3,2,1,0:T(8,128)(2,1)S(1)}, bf16[1,1,128,128]{3,2,1,0:T(8,128)(2,1)}, u32[]{:S(2)}) copy-start(bf16[1,1,128,128]{3,2,1,0:T(8,128)(2,1)} %param.17) | copy-start | bytes 98308
  6.2 0.7 %copy-start.10 = (s32[1,1,4]{2,1,0:T(1,128)S(1)}, s32[1,1,4]{2,1,0:T(1,128)}, u32[]{:S(2)}) copy-start(s32[1,1,4]{2,1,0:T(1,128)} %param.13) | copy-start | bytes 52
  6.8 4.5 %copy-start.1 = (bf16[1,1,4,1152,128]{4,3,2,1,0:T(8,128)(2,1)S(1)}, bf16[1,1,4,1152,128]{4,3,2,1,0:T(8,128)(2,1)}, u32[]{:S(2)}) copy-start(bf16[1,1,4,1152,128]{4,3,2,1,0:T(8,128)(2,1)} %param.23) | copy-start | bytes 3538948
  6.8 4.5 %copy-start.3 = (bf16[1,1,128,9,128]{4,2,3,1,0:T(8,128)(2,1)S(1)}, bf16[1,1,128,9,128]{4,2,3,1,0:T(8,128)(2,1)}, u32[]{:S(2)}) copy-start(bf16[1,1,128,9,128]{4,2,3,1,0:T(8,128)(2,1)} %param.21) | copy-start | bytes 884740
  6.8 4.5 %copy-start.5 = (bf16[1,1,128,9,128]{4,2,3,1,0:T(8,128)(2,1)S(1)}, bf16[1,1,128,9,128]{4,2,3,1,0:T(8,128)(2,1)}, u32[]{:S(2)}) copy-start(bf16[1,1,128,9,128]{4,2,3,1,0:T(8,128)(2,1)} %param.22) | copy-start | bytes 884740
  11.2 13.5 %copy-start.8 = (bf16[1,1,128,128]{3,2,1,0:T(8,128)(2,1)S(1)}, bf16[1,1,128,128]{3,2,1,0:T(8,128)(2,1)}, u32[]{:S(2)}) copy-start(bf16[1,1,128,128]{3,2,1,0:T(8,128)(2,1)} %param.16) | copy-start | bytes 98308
  15.0 14.3 %copy-start.9 = (s32[1,1,2,128]{3,2,1,0:T(2,128)S(1)}, s32[1,1,2,128]{3,2,1,0:T(2,128)}, u32[]{:S(2)}) copy-start(s32[1,1,2,128]{3,2,1,0:T(2,128)} %param.15) | copy-start | bytes 3076
  15.0 14.3 %collective-permute-start = (bf16[1152,128]{1,0:T(8,128)(2,1)S(1)}, bf16[1152,128]{1,0:T(8,128)(2,1)S(1)}, u32[]{:S(2)}, u32[]{:S(2)}) collective-permute-start(bf16[1152,128]{1,0:T(8,128)(2,1)S(1)} %get-tuple-element.32), channel_id=1, source_target_pairs={{1,0},{2,1},{3,2},{4,3},{5,4},{6,5},{7,6},{8,7},{9,8},{10,9},{11,1... | collective-permute-start | bytes 884744 | tf_op jit(solution)/shard_map/ppermute | solution.py:420
  18.3 11.0 %collective-permute-start.1 = (bf16[1152,128]{1,0:T(8,128)(2,1)S(1)}, bf16[1152,128]{1,0:T(8,128)(2,1)S(1)}, u32[]{:S(2)}, u32[]{:S(2)}) collective-permute-start(bf16[1152,128]{1,0:T(8,128)(2,1)S(1)} %get-tuple-element.34), channel_id=1, source_target_pairs={{16,0},{32,16},{48,32},{64,48},{80,64},{96,80},{112,96},{128,112},... | collective-permute-start | bytes 884744 | tf_op jit(solution)/shard_map/ppermute | solution.py:420
  37.6 9.2 %collective-permute-start.2 = (bf16[1152,128]{1,0:T(8,128)(2,1)S(1)}, bf16[1152,128]{1,0:T(8,128)(2,1)S(1)}, u32[]{:S(2)}, u32[]{:S(2)}) collective-permute-start(bf16[1152,128]{1,0:T(8,128)(2,1)S(1)} %get-tuple-element.35.left), channel_id=1, source_target_pairs={{15,0},{0,1},{1,2},{2,3},{3,4},{4,5},{5,6},{6,7},{7,8},{8,9},{9,10... | collective-permute-start | bytes 884744 | tf_op jit(solution)/shard_map/ppermute | solution.py:420
  41.4 13.3 %collective-permute-start.3 = (bf16[1152,128]{1,0:T(8,128)(2,1)S(1)}, bf16[1152,128]{1,0:T(8,128)(2,1)S(1)}, u32[]{:S(2)}, u32[]{:S(2)}) collective-permute-start(bf16[1152,128]{1,0:T(8,128)(2,1)S(1)} %get-tuple-element.36.top), channel_id=1, source_target_pairs={{240,0},{0,16},{16,32},{32,48},{48,64},{64,80},{80,96},{96,112},{1... | collective-permute-start | bytes 884744 | tf_op jit(solution)/shard_map/ppermute | solution.py:420

commit v2 on v1

--- a/solution.py
+++ b/solution.py
@@ -18,6 +18,7 @@
 CHUNKS = CHI // GROUP
 ROWS = GROUP * 8
 VMEM = 24 * 1024 * 1024
+WORK = (10_000_000,) * 5
 
 
 def dot(a, b):
@@ -120,24 +121,37 @@
     return mask(leg_r, leg_u), mask(leg_d, leg_l), mask(leg_r, leg_d), mask(leg_u, leg_l)
 
 
-def kept_rows(site, phys, virt):
-    lane = lax.broadcasted_iota(jnp.int32, (4, 81), 1)
-    state = lax.broadcasted_iota(jnp.int32, (4, 81), 0)
+def kept_rows(site, phys, virt, corner):
+    lane = lax.broadcasted_iota(jnp.int32, (8, 81), 1)
+    state = lax.broadcasted_iota(jnp.int32, (8, 81), 0)
     leg_l = (lane * 19) >> 9
     rest = lane - 27 * leg_l
     leg_u = (rest * 57) >> 9
     rest = rest - 9 * leg_u
     leg_r = (rest * 11) >> 5
     leg_d = rest - 3 * leg_r
-    total = jnp.zeros((4, 81), jnp.int32)
+    total = jnp.zeros((8, 81), jnp.int32)
     for s in range(4):
-        total = total + jnp.where(state == s, phys[s], 0)
+        total = total + jnp.where(state == s, phys[0, 0, s], 0)
     for i in range(3):
         total = total + jnp.where(leg_l == i, virt[i, 0, 0], 0)
         total = total + jnp.where(leg_u == i, virt[i, 0, 1], 0)
         total = total - jnp.where(leg_r == i, virt[i, 0, 2], 0)
         total = total - jnp.where(leg_d == i, virt[i, 0, 3], 0)
-    return jnp.where(total == 0, site[...].astype(F32), 0.0)
+    corner[...] = jnp.zeros_like(corner)
+    for n in range(27):
+        corner[8 * n : 8 * n + 4, 0:3] = site[n].astype(F32)
+    lane = lax.broadcasted_iota(jnp.int32, (CHI, 81), 1)
+    leg = lax.broadcasted_iota(jnp.int32, (CHI, 81), 0)
+    place = jnp.where(lane - 3 * ((lane * 683) >> 11) == leg, 1.0, 0.0).astype(BF16)
+    wide_site = dot(corner[...].astype(BF16), place)
+    block = lax.broadcasted_iota(jnp.int32, (216, 81), 0) >> 3
+    lane = lax.broadcasted_iota(jnp.int32, (216, 81), 1)
+    wide_site = jnp.where((lane * 683) >> 11 == block, wide_site, 0.0)
+    rows = wide_site[0:8]
+    for n in range(1, 27):
+        rows = rows + wide_site[8 * n : 8 * n + 8]
+    return jnp.where(total == 0, rows, 0.0)
 
 
 def build_layers(kept, out_a, out_b, out_c):
@@ -159,62 +173,64 @@
     out_c[...] = build(m_rd, m_ul)
 
 
-def unpack_term(wide, term):
+def unpack_term(wide, term, sent):
     for p in range(D2):
-        term[p * CHI : (p + 1) * CHI, :] = packed_slab(wide, p).astype(term.dtype)
-
-
-def right_kernel(
-    phys, virt, site, corner, edge_r, edge_t, sketches,
-    term, lay_a, lay_b, lay_c, pair_out, rows_t,
-    wide, thin, sketch, arrived,
+        part = packed_slab(wide, p)
+        term[p * CHI : (p + 1) * CHI, :] = part
+        sent[p * CHI : (p + 1) * CHI, :] = part.astype(BF16)
+
+
+def add_charges(sent, env, virt, leg):
+    sent[CUT : CUT + 16, :] = jnp.concatenate(
+        [env]
+        + [
+            jnp.full((1, CHI), (virt[p // 3, 0, leg] - virt[p % 3, 0, leg]).astype(F32))
+            for p in range(D2)
+        ]
+        + [jnp.zeros((6, CHI), F32)],
+        axis=0,
+    ).astype(BF16)
+
+
+def bring(sources, targets, arrived):
+    copies = [
+        pltpu.make_async_copy(source, target, arrived.at[i])
+        for i, (source, target) in enumerate(zip(sources, targets))
+    ]
+    for copy in copies:
+        copy.start()
+    return copies
+
+
+def upper_kernel(
+    phys_h, virt_h, site_h, env_h, corner_h, edge_t_h, edge_l_h, sketches,
+    own_left, own_top, sent_left, sent_top, corner_edge, corner_side, lay_a, lay_b,
+    phys, virt, site, env, corner, edge_t, edge_l, sketch_l, sketch_t, arrived,
+    left_rows, sketch_cols, sketch_rows, wide, thin, top_sum, lay_c, small,
 ):
-    coming = fetch(sketches, 3, sketch, arrived)
-    build_layers(kept_rows(site, phys, virt), lay_a, lay_b, lay_c)
-    pair_out[...] = dot(corner[...], side_by_side(edge_r)).astype(BF16)
-    pack_rows(lambda p: slab(edge_t, p), wide, rows_t)
-    coming.wait()
-
-    def consume(rows, block):
-        wide[rows, :] = dot(block, sketch[...])
-
-    chain(rows_t, pair_out, lay_a, thin, consume)
-    unpack_term(wide, term)
-
-
-def lower_kernel(
-    corner, edge_b, edge_l, lay_b, sketches,
-    term, pair_out, rows_l,
-    wide, thin, sketch, arrived,
-):
-    coming = fetch(sketches, 1, sketch, arrived)
-    pair_out[...] = dot(corner[...], side_by_side(edge_b)).astype(BF16)
-    pack_rows(lambda p: slab(edge_l, p), wide, rows_l)
-    coming.wait()
-
-    def consume(rows, block):
-        wide[rows, :] = dot(block, sketch[...])
-
-    chain(rows_l, pair_out, lay_b, thin, consume)
-    unpack_term(wide, term)
-
-
-def upper_kernel(
-    corner, edge_t, edge_l, lay_c, sketches,
-    own_left, own_top, corner_edge, corner_side,
-    left_rows, sketch_cols, sketch_rows, wide, thin, top_sum,
-    sketch_l, sketch_t, arrived_l, arrived_t,
-):
-    coming_l = fetch(sketches, 0, sketch_l, arrived_l)
-    coming_t = fetch(sketches, 2, sketch_t, arrived_t)
+    first = sketches.at[pl.ds(0, CUT), :]
+    third_one = sketches.at[pl.ds(2 * CUT, CUT), :]
+    copies = bring(
+        (phys_h, virt_h, site_h, env_h, corner_h, edge_t_h, edge_l_h, first, third_one),
+        (phys, virt, site, env, corner, edge_t, edge_l, sketch_l, sketch_t),
+        arrived,
+    )
+    for copy in copies[:4]:
+        copy.wait()
+    build_layers(kept_rows(site, phys, virt, small), lay_a, lay_b, lay_c)
+    charges = env[...].astype(F32)
+    add_charges(sent_left, charges[0:1], virt, 3)
+    add_charges(sent_top, charges[1:2], virt, 2)
+    for copy in copies[4:7]:
+        copy.wait()
     corner_edge[...] = dot(corner[...], side_by_side(edge_t)).astype(BF16)
     corner_side[...] = dot_tn(corner[...], side_by_side(edge_l)).astype(BF16)
     pack_rows(lambda p: jnp.transpose(slab(edge_l, p).astype(F32)), wide, left_rows)
-    coming_l.wait()
+    copies[7].wait()
     wide[...] = sketch_l[...].astype(F32)
     for p in range(D2):
         sketch_cols[p * CHI : (p + 1) * CHI, :] = wide[pl.ds(p, CHI, stride=D2), :].astype(BF16)
-    coming_t.wait()
+    copies[8].wait()
     wide[...] = sketch_t[...].astype(F32)
     picked = [wide[pl.ds(p, CHI, stride=D2), :] for p in range(D2)]
     pack_rows(lambda p: picked[p], wide, sketch_rows)
@@ -225,9 +241,34 @@
         top_sum[...] += dot_tn(sketch_rows[rows, :], block)
 
     chain(left_rows, corner_edge, lay_c, thin, consume)
-    unpack_term(wide, own_left)
+    unpack_term(wide, own_left, sent_left)
     for p in range(D2):
-        own_top[p * CHI : (p + 1) * CHI, :] = jnp.transpose(top_sum[:, p * CHI : (p + 1) * CHI])
+        part = jnp.transpose(top_sum[:, p * CHI : (p + 1) * CHI])
+        own_top[p * CHI : (p + 1) * CHI, :] = part
+        sent_top[p * CHI : (p + 1) * CHI, :] = part.astype(BF16)
+
+
+def other_kernel(
+    which, layer, corner_h, edge_h, edge_rows_h, sketches,
+    term, sent, pair_out, rows_out,
+    corner, edge, edge_rows, sketch, arrived, wide, thin,
+):
+    copies = bring(
+        (corner_h, edge_h, edge_rows_h, sketches.at[pl.ds(which * CUT, CUT), :]),
+        (corner, edge, edge_rows, sketch),
+        arrived,
+    )
+    for copy in copies[:3]:
+        copy.wait()
+    pair_out[...] = dot(corner[...], side_by_side(edge)).astype(BF16)
+    pack_rows(lambda p: slab(edge_rows, p), wide, rows_out)
+    copies[3].wait()
+
+    def consume(rows, block):
+        wide[rows, :] = dot(block, sketch[...])
+
+    chain(rows_out, pair_out, layer, thin, consume)
+    unpack_term(wide, term, sent)
 
 
 BLOCK = 32
@@ -309,109 +350,111 @@
     return [jnp.concatenate(i, axis=0) for i in inv]
 
 
-def basis_kernel(virt, env, own_left, below, own_top, beside, left_out, top_out, range_l, range_t):
+def halves(values):
+    high = values.astype(BF16)
+    return high, (values - high.astype(F32)).astype(BF16)
+
+
+def gram_of(ranged):
+    high, low = halves(ranged)
+    cross = dot_tn(high, low)
+    return dot_tn(high, high) + (cross + jnp.transpose(cross))
+
+
+def times_inverse(ranged, inverse):
+    high, low = halves(ranged)
+    inv_high, inv_low = halves(inverse)
+    return dot_nt(high, inv_high) + (dot_nt(high, inv_low) + dot_nt(low, inv_high))
+
+
+def unit(values):
+    square = jnp.sum(jnp.sum(values * values, axis=1, keepdims=True), axis=0, keepdims=True)
+    return (values / jnp.sqrt(square / values.size + 1e-06)).astype(BF16)
+
+
+def slab_rows(wide_ref, p):
+    return wide_ref[:, p * CHI : (p + 1) * CHI]
+
+
+def corner_from(projector, pair):
+    tall = jnp.concatenate([slab_rows(pair, p) for p in range(D2)], axis=0)
+    return dot_tn(projector[...], tall)
+
+
+def bond_kernel(
+    side, leg, virt_h, env_h, own, own_other, near, far, natural, layer, pair_own, pair_far,
+    out_own, out_edge, out_far,
+    virt, env, arrived, ranged, basis_own, basis_far, beside, packed, wide, thin, total,
+):
+    copies = bring((virt_h, env_h), (virt, env), arrived)
+    for copy in copies:
+        copy.wait()
     row = lax.broadcasted_iota(jnp.int32, (CHI, CHI), 0)
     col = lax.broadcasted_iota(jnp.int32, (CHI, CHI), 1)
     grams = []
-    for side, (own, other, ranged, leg) in enumerate(
-        ((own_left, below, range_l, 3), (own_top, beside, range_t, 2))
-    ):
-        across = jnp.broadcast_to(env[side : side + 1, :].astype(F32), (CHI, CHI))
+    for which in range(2):
+        if which == 0:
+            first, second = own, near
+            charges = env[side : side + 1, :].astype(F32)
+            shifts = [
+                (virt[p // 3, 0, leg] - virt[p % 3, 0, leg]).astype(F32) for p in range(D2)
+            ]
+        else:
+            first, second = own_other, far
+            tags = far[CUT : CUT + 16, :].astype(F32)
+            charges = tags[0:1]
+            shifts = [tags[1 + p : 2 + p] for p in range(D2)]
+        across = jnp.broadcast_to(charges, (CHI, CHI))
         gap = across - jnp.transpose(across)
         for p in range(D2):
-            shift = (virt[p // 3, 0, leg] - virt[p % 3, 0, leg]).astype(F32)
-            total = slab(own, p) + slab(other, p).astype(F32)
-            ranged[p * CHI : (p + 1) * CHI, :] = jnp.where(gap == shift, total, 0.0)
-        gram = exact_tn(ranged[...], ranged[...])
+            sums = slab(first, p) + slab(second, p).astype(F32)
+            ranged[which * CUT + p * CHI : which * CUT + (p + 1) * CHI, :] = jnp.where(
+                gap == shifts[p], sums, 0.0
+            )
+        gram = gram_of(ranged[which * CUT : (which + 1) * CUT, :])
         diagonal = jnp.where(row == col, gram, 0.0)
         mean = jnp.sum(jnp.sum(diagonal, axis=1, keepdims=True), axis=0, keepdims=True) / CHI
         grams.append(gram + jnp.where(row == col, 0.01 * mean + 1e-06, 0.0))
     inverses = eliminate(grams)
-    left_out[...] = exact_nt(range_l[...], inverses[0]).astype(BF16)
-    top_out[...] = exact_nt(range_t[...], inverses[1]).astype(BF16)
-
-
-def unit(values):
-    square = jnp.sum(jnp.sum(values * values, axis=1, keepdims=True), axis=0, keepdims=True)
-    return (values / jnp.sqrt(square / values.size + 1e-06)).astype(BF16)
-
-
-def slab_rows(wide_ref, p):
-    return wide_ref[:, p * CHI : (p + 1) * CHI]
-
-
-def corner_from(projector, pair):
-    tall = jnp.concatenate([slab_rows(pair, p) for p in range(D2)], axis=0)
-    return dot_tn(projector[...], tall)
-
-
-def own_kernel(
-    left, top, rows_l, rows_t, lay_a, lay_b, lower_pair, right_pair,
-    out_ll, out_tr, mixed_l, mixed_t,
-    beside, thin,
-):
-    for own, natural, layer, mixed in ((left, rows_l, lay_b, mixed_l), (top, rows_t, lay_a, mixed_t)):
-        beside[...] = side_by_side(own)
-
-        def consume(rows, block):
-            mixed[rows, :] = block
-
-        chain(natural, beside, layer, thin, consume)
-    out_ll[...] = unit(corner_from(left, lower_pair))
-    out_tr[...] = unit(corner_from(top, right_pair))
-
-
-def final_kernel(
-    above, before, mixed_l, mixed_t, corner_edge, corner_side,
-    out_lu, out_le, out_tl, out_te,
-    packed, wide,
-):
-    for other, mixed, out in ((above, mixed_l, out_le), (before, mixed_t, out_te)):
-        pack_rows(lambda p: slab(other, p), wide, packed)
-        result = unit(dot_tn(packed[...], mixed[...]))
-        for p in range(D2):
-            out[p * CHI : (p + 1) * CHI, :] = result[:, p * CHI : (p + 1) * CHI]
-    out_lu[...] = unit(corner_from(above, corner_edge))
-    out_tl[...] = unit(jnp.transpose(corner_from(before, corner_side)))
+    basis_own[...] = times_inverse(ranged[0:CUT, :], inverses[0]).astype(BF16)
+    basis_far[...] = times_inverse(ranged[CUT : 2 * CUT, :], inverses[1]).astype(BF16)
+    beside[...] = side_by_side(basis_own)
+    pack_rows(lambda p: slab(basis_far, p), wide, packed)
+    total[...] = jnp.zeros_like(total)
+
+    def consume(rows, block):
+        total[...] += dot_tn(packed[rows, :], block)
+
+    chain(natural, beside, layer, thin, consume)
+    result = unit(total[...])
+    for p in range(D2):
+        out_edge[p * CHI : (p + 1) * CHI, :] = result[:, p * CHI : (p + 1) * CHI]
+    out_own[...] = unit(corner_from(basis_own, pair_own))
+    far_corner = corner_from(basis_far, pair_far)
+    out_far[...] = unit(jnp.transpose(far_corner) if side else far_corner)
 
 
 def shape(*dims, dtype=BF16):
     return jax.ShapeDtypeStruct(dims, dtype)
 
 
-def vmem_in(count):
-    return [pl.BlockSpec(memory_space=pltpu.VMEM)] * count
-
-
-def smem_in(count):
-    return [pl.BlockSpec(memory_space=pltpu.SMEM)] * count
-
-
-def fetch(sketches, index, buffer, arrived):
-    copy = pltpu.make_async_copy(sketches.at[pl.ds(index * CUT, CUT), :], buffer, arrived)
-    copy.start()
-    return copy
-
-
-def call(body, name, smem, ins, outs, scratch, flops, fetches=0):
+def call(body, name, ins, outs, scratch, flops, far=()):
     moved = sum(a.size * a.dtype.itemsize for a in ins) + sum(
         o.size * jnp.dtype(o.dtype).itemsize for o in outs
     )
-    specs = vmem_in(len(ins))
-    buffers = [pltpu.VMEM(s, d) for s, d in scratch]
-    if fetches:
-        specs[-1] = pl.BlockSpec(memory_space=pl.ANY)
-        buffers += [pltpu.VMEM((CUT, CHI), BF16)] * fetches + [pltpu.SemaphoreType.DMA] * fetches
+    whole = pl.BlockSpec(memory_space=pltpu.VMEM)
     return pl.pallas_call(
         body,
         name=name,
         out_shape=tuple(outs),
-        in_specs=smem_in(len(smem)) + specs,
-        out_specs=tuple(vmem_in(len(outs))),
-        scratch_shapes=buffers,
-        compiler_params=pltpu.CompilerParams(vmem_limit_bytes=VMEM),
+        in_specs=[
+            pl.BlockSpec(memory_space=pltpu.HBM) if i in far else whole for i in range(len(ins))
+        ],
+        out_specs=(whole,) * len(outs),
+        scratch_shapes=scratch,
+        compiler_params=pltpu.CompilerParams(vmem_limit_bytes=VMEM if name != "upper" else 60 * 1024 * 1024),
         cost_estimate=pl.CostEstimate(flops=flops, bytes_accessed=moved, transcendentals=0),
-    )(*smem, *ins)
+    )(*ins)
 
 
 def from_behind(block, axis, distance):
@@ -420,9 +463,6 @@
     return lax.ppermute(block, axis, route)
 
 
-SEND = BF16
-
-
 def flat(edge):
     return edge.transpose(1, 0, 2).reshape(CUT, CHI)
 
@@ -431,52 +471,60 @@
     site_tensor, phys_charge, virt_charge, env_charge, corner_ul, corner_ur, corner_ll,
     edge_top, edge_right, edge_bottom, edge_left, sketch,
 ):
-    site = site_tensor[0, 0].reshape(4, 81)
-    phys, env = phys_charge[0, 0], env_charge[0, 0]
-    virt = virt_charge[0, 0].T[:, None, :]
+    site = site_tensor.transpose(0, 1, 3, 4, 5, 2, 6).reshape(27, 4, 3)
+    virt = virt_charge.transpose(0, 3, 1, 2).reshape(3, 1, 4)
+    env = env_charge[0, 0]
     ul, ur, ll = corner_ul[0, 0], corner_ur[0, 0], corner_ll[0, 0]
     top, right, bottom, left = (
         flat(e[0, 0]) for e in (edge_top, edge_right, edge_bottom, edge_left)
     )
     sketches = sketch[0, 0].reshape(4 * CUT, CHI)
     tall = shape(CUT, CHI)
+    tall_wide = shape(CUT, CHI, dtype=F32)
+    tagged = shape(CUT + 16, CHI)
     broad = shape(CHI, CUT)
     lay = shape(LAY, LAY)
-    wide = ((CUT, CHI), F32)
-    thin = ((CHI * 16, CHI), F32)
-    square = shape(CUT, CUT)
-    work = 1_000_000_000
-    from_right, lay_a, lay_b, lay_c, right_pair, rows_t = call(
-        right_kernel, "right", [phys, virt], [site, ur, right, top, sketches],
-        [shape(CUT, CHI, dtype=SEND), lay, lay, lay, broad, tall], [wide, thin], work, 1,
-    )
-    beside = from_behind(from_right, "lx", -1)
-    from_lower, lower_pair, rows_l = call(
-        lower_kernel, "lower", [], [ll, bottom, left, lay_b, sketches],
-        [shape(CUT, CHI, dtype=SEND), broad, tall], [wide, thin], work, 1,
-    )
-    below = from_behind(from_lower, "ly", -1)
-    own_left, own_top, corner_edge, corner_side = call(
-        upper_kernel, "upper", [], [ul, top, left, lay_c, sketches],
-        [shape(CUT, CHI, dtype=F32), shape(CUT, CHI, dtype=F32), broad, broad],
-        [((CUT, CHI), BF16), ((CUT, CHI), BF16), ((CUT, CHI), BF16), wide, thin, ((CHI, CUT), F32)],
-        work, 2,
-    )
-    left_basis, top_basis = call(
-        basis_kernel, "basis", [virt], [env, own_left, below, own_top, beside], [tall, tall],
-        [((CUT, CHI), F32), ((CUT, CHI), F32)], work,
-    )
-    before = from_behind(top_basis, "lx", 1)
-    above = from_behind(left_basis, "ly", 1)
     corner = shape(CHI, CHI)
-    lo, tr, mixed_l, mixed_t = call(
-        own_kernel, "own", [],
-        [left_basis, top_basis, rows_l, rows_t, lay_a, lay_b, lower_pair, right_pair],
-        [corner, corner, square, square], [((CHI, CUT), BF16), thin], work,
-    )
-    lu, le, tl, te = call(
-        final_kernel, "final", [], [above, before, mixed_l, mixed_t, corner_edge, corner_side],
-        [corner, tall, corner, tall], [((CUT, CHI), BF16), wide], work,
+    keep = lambda *dims, dtype=BF16: pltpu.VMEM(dims, dtype)
+    slabs = keep(CUT, CHI)
+    wide = keep(CUT, CHI, dtype=F32)
+    thin = keep(CHI * 16, CHI, dtype=F32)
+    row_sum = keep(CHI, CUT, dtype=F32)
+    phys_s = pltpu.SMEM((1, 1, 4), jnp.int32)
+    virt_s = pltpu.SMEM((3, 1, 4), jnp.int32)
+    env_v = keep(2, CHI, dtype=jnp.int32)
+    arrivals = lambda n: pltpu.SemaphoreType.DMA((n,))
+    own_left, own_top, sent_left, sent_top, corner_edge, corner_side, lay_a, lay_b = call(
+        upper_kernel, "upper", [phys_charge, virt, site, env, ul, top, left, sketches],
+        [tall_wide, tall_wide, tagged, tagged, broad, broad, lay, lay],
+        [phys_s, virt_s, keep(27, 4, 3), env_v, keep(CHI, CHI), slabs, slabs, slabs, slabs, arrivals(9),
+         slabs, slabs, slabs, wide, thin, row_sum, keep(LAY, LAY), keep(216, CHI, dtype=F32)],
+        WORK[0], range(8),
+    )
+    before_range = from_behind(sent_top, "lx", 1)
+    above_range = from_behind(sent_left, "ly", 1)
+    others = [keep(CHI, CHI), slabs, slabs, slabs, arrivals(4), wide, thin]
+    from_lower, sent_lower, lower_pair, rows_l = call(
+        functools.partial(other_kernel, 1), "lower", [lay_b, ll, bottom, left, sketches],
+        [tall_wide, tall, broad, tall], others, WORK[1], range(1, 5),
+    )
+    below = from_behind(sent_lower, "ly", -1)
+    from_right, sent_right, right_pair, rows_t = call(
+        functools.partial(other_kernel, 3), "right", [lay_a, ur, right, top, sketches],
+        [tall_wide, tall, broad, tall], others, WORK[2], range(1, 5),
+    )
+    beside = from_behind(sent_right, "lx", -1)
+    bond = [virt_s, env_v, arrivals(2), keep(2 * CUT, CHI, dtype=F32), slabs, slabs,
+            keep(CHI, CUT), slabs, wide, thin, row_sum]
+    lo, le, lu = call(
+        functools.partial(bond_kernel, 0, 3), "left",
+        [virt, env, own_left, from_lower, below, above_range, rows_l, lay_b, lower_pair, corner_edge],
+        [corner, tall, corner], bond, WORK[3], range(2),
+    )
+    tr, te, tl = call(
+        functools.partial(bond_kernel, 1, 2), "top",
+        [virt, env, own_top, from_right, beside, before_range, rows_t, lay_a, right_pair, corner_side],
+        [corner, tall, corner], bond, WORK[4], range(2),
     )
     lift = lambda a: a[None, None]
     edge = lambda a: a.reshape(D2, CHI, CHI).transpose(1, 0, 2)[None, None]

time: 57.5 us -> 52.2 us (0.908)
  the two profiles are of different devices: /device:TPU:1 before, /device:TPU:8 now
where the time goes in v2:
time: 52.2 us; the launch traced here: 52 us
  Pallas kernels  38.3 us (73%)
  starting transfers between devices  11.9 us (23%)
  between operations  1.04 us (2%)
  local copies, waits for them, and re-layouts  0.8 us (2%)
    pallas_call x5, Pallas kernels, call(): pl.pallas_call(body, name=name, out_shape=tuple(outs), in_specs=[pl.Block...  38.3 us
    ppermute x4, starting transfers between devices, from_behind(): return lax.ppermute(block, axis, route)  11.9 us
  transfers between devices with their start and end apart: 4, of which 0 were waited for; matrix products, arithmetic and copies ran while one was open for 0% of the time, Pallas kernels for 37%

profile of v2, /device:TPU:8, one launch (start us, length us, event | category | flops | bytes accessed | tf_op | source)
XLA Modules:
  0.0 52.0 jit_solution(7940620850679020870)
XLA Ops:
  0.7 7.0 %upper.1 = (f32[1152,128]{1,0:T(8,128)}, f32[1152,128]{1,0:T(8,128)}, bf16[1168,128]{1,0:T(8,128)(2,1)}, bf16[1168,128]{1,0:T(8,128)(2,1)}, bf16[128,1152]{1,0:T...) custom-call(s32[1,1,4]{2,1,0:T(1,128)} %phys_h.1, s32[3,1,4]{2,1,0:T(1,128)} %bitcast.56, ...), custom_call_target="tpu_custom_call" | custom-call | flops 10000000 | bytes 4208328 | tf_op jit(solution)/shard_map/upper/pallas_call | solution.py:446
  7.6 0.0 copy-start.2
  7.7 0.0 copy-start.8
  7.7 0.0 copy-start.9
  7.7 0.1 collective-permute-start.1
  7.8 2.0 %collective-permute-start.3 = (bf16[1168,128]{1,0:T(8,128)(2,1)}, bf16[1168,128]{1,0:T(8,128)(2,1)S(1)}, u32[]{:S(2)}, u32[]{:S(2)}) collective-permute-start(bf16[1168,128]{1,0:T(8,128)(2,1)} %get-tuple-element.43), channel_id=1, source_target_pairs={{240,0},{0,16},{16,32},{32,48},{48,64},{64,80},{80,96},{96,112},{1... | collective-permute-start | bytes 897032 | tf_op jit(solution)/shard_map/ppermute | solution.py:463
  9.8 0.0 copy-done
  9.8 0.0 copy-start.10
  9.8 0.7 %copy-done.10 = bf16[96,96]{1,0:T(8,128)(2,1)S(1)} copy-done((bf16[96,96]{1,0:T(8,128)(2,1)S(1)}, bf16[96,96]{1,0:T(8,128)(2,1)}, u32[]{:S(2)}) %copy-start.10) | copy-done | bytes 18456
  10.5 3.9 %lower.1 = (f32[1152,128]{1,0:T(8,128)S(1)}, bf16[1152,128]{1,0:T(8,128)(2,1)S(1)}, bf16[128,1152]{1,0:T(8,128)(2,1)S(1)}, bf16[1152,128]{1,0:T(8,128)(2,1)S(1)}) custom-call(bf16[96,96]{1,0:T(8,128)(2,1)S(1)} %copy-done.10, bf16[128,128]{1,0:T(8,128)(2,1)S(1)} %bitcast.54, bf16[1152,128]{1,0:T(8,128)(2,1)S(1)} %bitcast.52, bf16[1152,128]{1,0:T(8,128)(2,1)S(1)} %bitcast.49, ...), custom_call_target="tpu_custom_call" | custom-call | flops 10000000 | bytes 3295232 | tf_op jit(solution)/shard_map/lower/pallas_call | solution.py:446
  14.4 0.0 copy-start.6
  14.5 0.0 copy-start.13
  14.5 0.0 copy-start.14
  14.5 3.8 %collective-permute-start = (bf16[1152,128]{1,0:T(8,128)(2,1)S(1)}, bf16[1152,128]{1,0:T(8,128)(2,1)S(1)}, u32[]{:S(2)}, u32[]{:S(2)}) collective-permute-start(bf16[1152,128]{1,0:T(8,128)(2,1)S(1)} %get-tuple-element.31), channel_id=1, source_target_pairs={{1,0},{2,1},{3,2},{4,3},{5,4},{6,5},{7,6},{8,7},{9,8},{10,9},{11,1... | collective-permute-start | bytes 884744 | tf_op jit(solution)/shard_map/ppermute | solution.py:463
  18.2 0.0 copy-done.12
  18.3 0.0 copy-done.8
  18.3 4.0 %right.1 = (f32[1152,128]{1,0:T(8,128)S(1)}, bf16[1152,128]{1,0:T(8,128)(2,1)S(1)}, bf16[128,1152]{1,0:T(8,128)(2,1)S(1)}, bf16[1152,128]{1,0:T(8,128)(2,1)S(1)}) custom-call(bf16[96,96]{1,0:T(8,128)(2,1)S(1)} %copy-done.9, bf16[128,128]{1,0:T(8,128)(2,1)S(1)} %bitcast.55, bf16[1152,128]{1,0:T(8,128)(2,1)S(1)} %bitcast.53, bf16[1152,128]{1,0:T(8,128)(2,1)S(1)} %bitcast.51, ...), custom_call_target="tpu_custom_call" | custom-call | flops 10000000 | bytes 3295232 | tf_op jit(solution)/shard_map/right/pallas_call | solution.py:446
  22.2 6.0 %collective-permute-start.2 = (bf16[1152,128]{1,0:T(8,128)(2,1)S(1)}, bf16[1152,128]{1,0:T(8,128)(2,1)S(1)}, u32[]{:S(2)}, u32[]{:S(2)}) collective-permute-start(bf16[1152,128]{1,0:T(8,128)(2,1)S(1)} %get-tuple-element.42), channel_id=1, source_target_pairs={{16,0},{32,16},{48,32},{64,48},{80,64},{96,80},{112,96},{128,112},... | collective-permute-start | bytes 884744 | tf_op jit(solution)/shard_map/ppermute | solution.py:463
  28.3 0.0 collective-permute-done.near
  28.3 0.0 collective-permute-done.1.far
  28.3 11.6 %left.1 = (bf16[128,128]{1,0:T(8,128)(2,1)}, bf16[1152,128]{1,0:T(8,128)(2,1)}, bf16[128,128]{1,0:T(8,128)(2,1)}) custom-call(s32[3,1,4]{2,1,0:T(1,128)S(1)} %bitcast.57, s32[2,128]{1,0:T(2,128)S(1)} %bitcast.60, f32[1152,128]{1,0:T(8,128)S(1)} %copy-done.4, f32[1152,128]{1,0:T(8,128)S(1)} %get-tuple-element.30.own_other, ...), custom_call_target="tpu_custom_call" | custom-call | flops 10000000 | bytes 3038256 | tf_op jit(solution)/shard_map/left/pallas_call | solution.py:446
  39.9 0.0 collective-permute-done.2.near
  39.9 0.0 collective-permute-done.3.far
  39.9 11.9 %top.1 = (bf16[128,128]{1,0:T(8,128)(2,1)}, bf16[1152,128]{1,0:T(8,128)(2,1)}, bf16[128,128]{1,0:T(8,128)(2,1)}) custom-call(s32[3,1,4]{2,1,0:T(1,128)S(1)} %bitcast.58, s32[2,128]{1,0:T(2,128)S(1)} %bitcast.61, f32[1152,128]{1,0:T(8,128)S(1)} %copy-done.3, f32[1152,128]{1,0:T(8,128)S(1)} %get-tuple-element.41.own_other, ...), custom_call_target="tpu_custom_call" | custom-call | flops 10000000 | bytes 3038256 | tf_op jit(solution)/shard_map/top/pallas_call | solution.py:446
  (19 shorter events, 0.0 us)
Async XLA Ops:
  0.6 9.1 %copy-start = (bf16[1,1,4,1152,128]{4,3,2,1,0:T(8,128)(2,1)S(1)}, bf16[1,1,4,1152,128]{4,3,2,1,0:T(8,128)(2,1)}, u32[]{:S(2)}) copy-start(bf16[1,1,4,1152,128]{4,3,2,1,0:T(8,128)(2,1)} %param.23) | copy-start | bytes 3538948
  0.6 9.1 %copy-start.1 = (bf16[1,1,128,9,128]{4,2,3,1,0:T(8,128)(2,1)S(1)}, bf16[1,1,128,9,128]{4,2,3,1,0:T(8,128)(2,1)}, u32[]{:S(2)}) copy-start(bf16[1,1,128,9,128]{4,2,3,1,0:T(8,128)(2,1)} %param.22) | copy-start | bytes 884740
  0.7 9.1 %copy-start.7 = (bf16[1,1,128,9,128]{4,2,3,1,0:T(8,128)(2,1)S(1)}, bf16[1,1,128,9,128]{4,2,3,1,0:T(8,128)(2,1)}, u32[]{:S(2)}) copy-start(bf16[1,1,128,9,128]{4,2,3,1,0:T(8,128)(2,1)} %param.21) | copy-start | bytes 884740
  0.7 9.1 %copy-start.11 = (bf16[1,1,128,128]{3,2,1,0:T(8,128)(2,1)S(1)}, bf16[1,1,128,128]{3,2,1,0:T(8,128)(2,1)}, u32[]{:S(2)}) copy-start(bf16[1,1,128,128]{3,2,1,0:T(8,128)(2,1)} %param.18) | copy-start | bytes 98308
  0.7 17.6 %copy-start.12 = (bf16[1,1,128,128]{3,2,1,0:T(8,128)(2,1)S(1)}, bf16[1,1,128,128]{3,2,1,0:T(8,128)(2,1)}, u32[]{:S(2)}) copy-start(bf16[1,1,128,128]{3,2,1,0:T(8,128)(2,1)} %param.17) | copy-start | bytes 98308
  7.6 10.6 %copy-start.2 = (bf16[1,1,128,9,128]{4,2,3,1,0:T(8,128)(2,1)S(1)}, bf16[1,1,128,9,128]{4,2,3,1,0:T(8,128)(2,1)}, u32[]{:S(2)}) copy-start(bf16[1,1,128,9,128]{4,2,3,1,0:T(8,128)(2,1)} %param.19) | copy-start | bytes 884740
  7.7 10.6 %copy-start.8 = (bf16[1,1,128,9,128]{4,2,3,1,0:T(8,128)(2,1)S(1)}, bf16[1,1,128,9,128]{4,2,3,1,0:T(8,128)(2,1)}, u32[]{:S(2)}) copy-start(bf16[1,1,128,9,128]{4,2,3,1,0:T(8,128)(2,1)} %param.20) | copy-start | bytes 884740
  7.7 10.6 %copy-start.9 = (bf16[96,96]{1,0:T(8,128)(2,1)S(1)}, bf16[96,96]{1,0:T(8,128)(2,1)}, u32[]{:S(2)}) copy-start(bf16[96,96]{1,0:T(8,128)(2,1)} %get-tuple-element.40.layer) | copy-start | bytes 55300
  7.7 20.6 %collective-permute-start.1 = (bf16[1168,128]{1,0:T(8,128)(2,1)}, bf16[1168,128]{1,0:T(8,128)(2,1)S(1)}, u32[]{:S(2)}, u32[]{:S(2)}) collective-permute-start(bf16[1168,128]{1,0:T(8,128)(2,1)} %get-tuple-element.32), channel_id=1, source_target_pairs={{15,0},{0,1},{1,2},{2,3},{3,4},{4,5},{5,6},{6,7},{7,8},{8,9},{9,10... | collective-permute-start | bytes 897032 | tf_op jit(solution)/shard_map/ppermute | solution.py:463
  7.8 32.1 %collective-permute-start.3 = (bf16[1168,128]{1,0:T(8,128)(2,1)}, bf16[1168,128]{1,0:T(8,128)(2,1)S(1)}, u32[]{:S(2)}, u32[]{:S(2)}) collective-permute-start(bf16[1168,128]{1,0:T(8,128)(2,1)} %get-tuple-element.43), channel_id=1, source_target_pairs={{240,0},{0,16},{16,32},{32,48},{48,64},{64,80},{80,96},{96,112},{1... | collective-permute-start | bytes 897032 | tf_op jit(solution)/shard_map/ppermute | solution.py:463
  9.8 0.7 %copy-start.10 = (bf16[96,96]{1,0:T(8,128)(2,1)S(1)}, bf16[96,96]{1,0:T(8,128)(2,1)}, u32[]{:S(2)}) copy-start(bf16[96,96]{1,0:T(8,128)(2,1)} %get-tuple-element.29.layer) | copy-start | bytes 55300
  14.4 13.8 %copy-start.4 = (f32[1152,128]{1,0:T(8,128)S(1)}, f32[1152,128]{1,0:T(8,128)}, u32[]{:S(2)}) copy-start(f32[1152,128]{1,0:T(8,128)} %get-tuple-element.28.own) | copy-start | bytes 1769476
  14.4 13.8 %copy-start.6 = (bf16[128,1152]{1,0:T(8,128)(2,1)S(1)}, bf16[128,1152]{1,0:T(8,128)(2,1)}, u32[]{:S(2)}) copy-start(bf16[128,1152]{1,0:T(8,128)(2,1)} %get-tuple-element.35.pair_far) | copy-start | bytes 884740
  14.5 13.8 %copy-start.13 = (s32[1,1,4,3]{2,1,3,0:T(1,128)S(1)}, s32[1,1,4,3]{2,1,3,0:T(1,128)}, u32[]{:S(2)}) copy-start(s32[1,1,4,3]{2,1,3,0:T(1,128)} %param.14) | copy-start | bytes 148
  14.5 13.8 %copy-start.14 = (s32[1,1,2,128]{3,2,1,0:T(2,128)S(1)}, s32[1,1,2,128]{3,2,1,0:T(2,128)}, u32[]{:S(2)}) copy-start(s32[1,1,2,128]{3,2,1,0:T(2,128)} %param.15) | copy-start | bytes 3076
  14.5 13.8 %collective-permute-start = (bf16[1152,128]{1,0:T(8,128)(2,1)S(1)}, bf16[1152,128]{1,0:T(8,128)(2,1)S(1)}, u32[]{:S(2)}, u32[]{:S(2)}) collective-permute-start(bf16[1152,128]{1,0:T(8,128)(2,1)S(1)} %get-tuple-element.31), channel_id=1, source_target_pairs={{1,0},{2,1},{3,2},{4,3},{5,4},{6,5},{7,6},{8,7},{9,8},{10,9},{11,1... | collective-permute-start | bytes 884744 | tf_op jit(solution)/shard_map/ppermute | solution.py:463
  22.2 17.6 %collective-permute-start.2 = (bf16[1152,128]{1,0:T(8,128)(2,1)S(1)}, bf16[1152,128]{1,0:T(8,128)(2,1)S(1)}, u32[]{:S(2)}, u32[]{:S(2)}) collective-permute-start(bf16[1152,128]{1,0:T(8,128)(2,1)S(1)} %get-tuple-element.42), channel_id=1, source_target_pairs={{16,0},{32,16},{48,32},{64,48},{80,64},{96,80},{112,96},{128,112},... | collective-permute-start | bytes 884744 | tf_op jit(solution)/shard_map/ppermute | solution.py:463
  28.3 11.6 %copy-start.3 = (f32[1152,128]{1,0:T(8,128)S(1)}, f32[1152,128]{1,0:T(8,128)}, u32[]{:S(2)}) copy-start(f32[1152,128]{1,0:T(8,128)} %get-tuple-element.39.own) | copy-start | bytes 1769476
  28.3 11.6 %copy-start.5 = (bf16[128,1152]{1,0:T(8,128)(2,1)S(1)}, bf16[128,1152]{1,0:T(8,128)(2,1)}, u32[]{:S(2)}) copy-start(bf16[128,1152]{1,0:T(8,128)(2,1)} %get-tuple-element.46.pair_far) | copy-start | bytes 884740

commit v3 on v2

--- a/solution.py
+++ b/solution.py
@@ -18,7 +18,7 @@
 CHUNKS = CHI // GROUP
 ROWS = GROUP * 8
 VMEM = 24 * 1024 * 1024
-WORK = (10_000_000,) * 5
+WORK = 10_000_000
 
 
 def dot(a, b):
@@ -64,22 +64,47 @@
     return wide[pl.ds(p, CHI, stride=8), :] if p < 8 else wide[TALL:CUT, :]
 
 
+def weave(one, steps_one, two, steps_two):
+    done_one = done_two = 0
+    live_one = live_two = True
+    while live_one or live_two:
+        if live_one and (not live_two or done_one * steps_two <= done_two * steps_one):
+            live_one = next(one, "end") != "end"
+            done_one += 1
+        else:
+            live_two = next(two, "end") != "end"
+            done_two += 1
+
+
+def run(steps):
+    for _ in steps:
+        pass
+
+
+CHAIN_STEPS = 3 * CHUNKS + 2
+
+
 def chain(left, right, layer, thin, consume):
     thin[...] = jnp.zeros_like(thin)
     last = dot(left[TALL:CUT, :], right[...])
     for q in range(D2):
         thin[pl.ds(q, CHI, stride=16), :] = last[:, q * CHI : (q + 1) * CHI]
+    yield
     blank = jnp.zeros((8, CHI), F32)
-    for chunk in range(CHUNKS):
-        rows = slice(chunk * ROWS, (chunk + 1) * ROWS)
-        three = dot(left[rows, :], right[...])
+
+    def product(chunk):
+        return dot(left[chunk * ROWS : (chunk + 1) * ROWS, :], right[...])
+
+    def mix(chunk, three):
         stacks = []
         for f in range(GROUP):
             here = (chunk * GROUP + f) * 16
             parts = [three[f * 8 : f * 8 + 8, q * CHI : (q + 1) * CHI] for q in range(D2)]
             stack = jnp.concatenate(parts + [thin[here : here + 16, :], blank], axis=0)
             stacks.append(stack.astype(BF16))
-        mixed = dot(layer[...], jnp.concatenate(stacks, axis=1))
+        return dot(layer[...], jnp.concatenate(stacks, axis=1))
+
+    def hand_on(chunk, mixed):
         tall = []
         for f in range(GROUP):
             here = (chunk * GROUP + f) * 16
@@ -88,7 +113,21 @@
             tall.append(
                 jnp.concatenate([mixed[s * 8 : s * 8 + 8, lanes] for s in range(D2)], axis=1)
             )
+        rows = slice(chunk * ROWS, (chunk + 1) * ROWS)
         consume(rows, jnp.concatenate(tall, axis=0).astype(BF16))
+
+    three = product(0)
+    before = None
+    for chunk in range(CHUNKS):
+        following = product(chunk + 1) if chunk + 1 < CHUNKS else None
+        yield
+        mixed = mix(chunk, three)
+        yield
+        if before is not None:
+            hand_on(chunk - 1, before)
+        yield
+        before, three = mixed, following
+    hand_on(CHUNKS - 1, before)
     rest = [thin[pl.ds(s, CHI, stride=16), :].astype(BF16) for s in range(D2)]
     consume(slice(TALL, CUT), jnp.concatenate(rest, axis=1))
 
@@ -202,35 +241,78 @@
     return copies
 
 
+def right_kernel(
+    phys_h, virt_h, site_h, corner_h, edge_h, edge_rows_h, sketches,
+    term, sent, pair_out, rows_out, lay_a, lay_b, lay_c,
+    phys, virt, site, corner, edge, edge_rows, sketch, arrived, wide, thin, small,
+):
+    copies = bring(
+        (phys_h, virt_h, site_h, corner_h, edge_h, edge_rows_h, sketches.at[pl.ds(3 * CUT, CUT), :]),
+        (phys, virt, site, corner, edge, edge_rows, sketch),
+        arrived,
+    )
+    for copy in copies[:3]:
+        copy.wait()
+    build_layers(kept_rows(site, phys, virt, small), lay_a, lay_b, lay_c)
+    sent[CUT : CUT + 32, :] = jnp.zeros((32, CHI), BF16)
+    corner_product(copies[3:], corner, edge, edge_rows, sketch, lay_a, term, sent, pair_out, rows_out, wide, thin)
+
+
+def lower_kernel(
+    layer, corner_h, edge_h, edge_rows_h, sketches,
+    term, sent, pair_out,
+    corner, edge, edge_rows, sketch, arrived, wide, thin, rows_out,
+):
+    copies = bring(
+        (corner_h, edge_h, edge_rows_h, sketches.at[pl.ds(CUT, CUT), :]),
+        (corner, edge, edge_rows, sketch),
+        arrived,
+    )
+    corner_product(copies, corner, edge, edge_rows, sketch, layer, term, sent, pair_out, rows_out, wide, thin)
+
+
+def corner_product(
+    copies, corner, edge, edge_rows, sketch, layer, term, sent, pair_out, rows_out, wide, thin
+):
+    for copy in copies[:3]:
+        copy.wait()
+    pair_out[...] = dot(corner[...], side_by_side(edge)).astype(BF16)
+    pack_rows(lambda p: slab(edge_rows, p), wide, rows_out)
+    copies[3].wait()
+
+    def consume(rows, block):
+        wide[rows, :] = dot(block, sketch[...])
+
+    run(chain(rows_out, pair_out, layer, thin, consume))
+    unpack_term(wide, term, sent)
+
+
 def upper_kernel(
-    phys_h, virt_h, site_h, env_h, corner_h, edge_t_h, edge_l_h, sketches,
-    own_left, own_top, sent_left, sent_top, corner_edge, corner_side, lay_a, lay_b,
-    phys, virt, site, env, corner, edge_t, edge_l, sketch_l, sketch_t, arrived,
-    left_rows, sketch_cols, sketch_rows, wide, thin, top_sum, lay_c, small,
+    lay_c, virt_h, env_h, corner_h, edge_t_h, edge_l_h, sketches,
+    own_left, own_top, sent_left, sent_top, corner_edge, corner_side, left_rows,
+    virt, env, corner, edge_t, edge_l, sketch_l, sketch_t, arrived,
+    sketch_cols, sketch_rows, wide, thin, top_sum,
 ):
     first = sketches.at[pl.ds(0, CUT), :]
     third_one = sketches.at[pl.ds(2 * CUT, CUT), :]
     copies = bring(
-        (phys_h, virt_h, site_h, env_h, corner_h, edge_t_h, edge_l_h, first, third_one),
-        (phys, virt, site, env, corner, edge_t, edge_l, sketch_l, sketch_t),
+        (virt_h, env_h, corner_h, edge_t_h, edge_l_h, first, third_one),
+        (virt, env, corner, edge_t, edge_l, sketch_l, sketch_t),
         arrived,
     )
-    for copy in copies[:4]:
+    for copy in copies[:5]:
         copy.wait()
-    build_layers(kept_rows(site, phys, virt, small), lay_a, lay_b, lay_c)
     charges = env[...].astype(F32)
     add_charges(sent_left, charges[0:1], virt, 3)
     add_charges(sent_top, charges[1:2], virt, 2)
-    for copy in copies[4:7]:
-        copy.wait()
     corner_edge[...] = dot(corner[...], side_by_side(edge_t)).astype(BF16)
     corner_side[...] = dot_tn(corner[...], side_by_side(edge_l)).astype(BF16)
     pack_rows(lambda p: jnp.transpose(slab(edge_l, p).astype(F32)), wide, left_rows)
-    copies[7].wait()
+    copies[5].wait()
     wide[...] = sketch_l[...].astype(F32)
     for p in range(D2):
         sketch_cols[p * CHI : (p + 1) * CHI, :] = wide[pl.ds(p, CHI, stride=D2), :].astype(BF16)
-    copies[8].wait()
+    copies[6].wait()
     wide[...] = sketch_t[...].astype(F32)
     picked = [wide[pl.ds(p, CHI, stride=D2), :] for p in range(D2)]
     pack_rows(lambda p: picked[p], wide, sketch_rows)
@@ -240,7 +322,7 @@
         wide[rows, :] = dot(block, sketch_cols[...])
         top_sum[...] += dot_tn(sketch_rows[rows, :], block)
 
-    chain(left_rows, corner_edge, lay_c, thin, consume)
+    run(chain(left_rows, corner_edge, lay_c, thin, consume))
     unpack_term(wide, own_left, sent_left)
     for p in range(D2):
         part = jnp.transpose(top_sum[:, p * CHI : (p + 1) * CHI])
@@ -248,35 +330,11 @@
         sent_top[p * CHI : (p + 1) * CHI, :] = part.astype(BF16)
 
 
-def other_kernel(
-    which, layer, corner_h, edge_h, edge_rows_h, sketches,
-    term, sent, pair_out, rows_out,
-    corner, edge, edge_rows, sketch, arrived, wide, thin,
-):
-    copies = bring(
-        (corner_h, edge_h, edge_rows_h, sketches.at[pl.ds(which * CUT, CUT), :]),
-        (corner, edge, edge_rows, sketch),
-        arrived,
-    )
-    for copy in copies[:3]:
-        copy.wait()
-    pair_out[...] = dot(corner[...], side_by_side(edge)).astype(BF16)
-    pack_rows(lambda p: slab(edge_rows, p), wide, rows_out)
-    copies[3].wait()
-
-    def consume(rows, block):
-        wide[rows, :] = dot(block, sketch[...])
-
-    chain(rows_out, pair_out, layer, thin, consume)
-    unpack_term(wide, term, sent)
-
-
 BLOCK = 32
 
 
 def reciprocal(x):
     r = pl.reciprocal(x, approx=True)
-    r = r * (2.0 - x * r)
     return r * (2.0 - x * r)
 
 
@@ -284,7 +342,10 @@
     return jnp.broadcast_to(rows[p : p + 1, :], (8, CHI))
 
 
-def eliminate(grams):
+STEPS = CHI // 2
+
+
+def eliminate(grams, result):
     count = len(grams)
     sub = lax.broadcasted_iota(jnp.int32, (8, CHI), 0)
     lane = lax.broadcasted_iota(jnp.int32, (8, CHI), 1)
@@ -335,6 +396,7 @@
                             own[j] = own[j] - by_p * row_p[n] - by_q * row_q[n]
                         fact[m][g] = fact[m][g] - by_p * fact_p - by_q * fact_q
                         inv[m][g] = inv[m][g] - by_p * inv_p - by_q * inv_q
+                yield
             for m in range(count):
                 root = lax.rsqrt(pivots[m])
                 fact[m][b] = fact[m][b] * root
@@ -347,7 +409,7 @@
                 for g in range(end, groups):
                     fact[m][g] = fact[m][g] - update[8 * g : 8 * g + 8, :CHI]
                     inv[m][g] = inv[m][g] - update[8 * g : 8 * g + 8, CHI:]
-    return [jnp.concatenate(i, axis=0) for i in inv]
+    result.extend(jnp.concatenate(i, axis=0) for i in inv)
 
 
 def halves(values):
@@ -381,64 +443,83 @@
     return dot_tn(projector[...], tall)
 
 
-def bond_kernel(
-    side, leg, virt_h, env_h, own, own_other, near, far, natural, layer, pair_own, pair_far,
-    out_own, out_edge, out_far,
-    virt, env, arrived, ranged, basis_own, basis_far, beside, packed, wide, thin, total,
-):
-    copies = bring((virt_h, env_h), (virt, env), arrived)
-    for copy in copies:
-        copy.wait()
+def range_and_gram(own, other, tagged, ranged):
     row = lax.broadcasted_iota(jnp.int32, (CHI, CHI), 0)
     col = lax.broadcasted_iota(jnp.int32, (CHI, CHI), 1)
-    grams = []
-    for which in range(2):
-        if which == 0:
-            first, second = own, near
-            charges = env[side : side + 1, :].astype(F32)
-            shifts = [
-                (virt[p // 3, 0, leg] - virt[p % 3, 0, leg]).astype(F32) for p in range(D2)
-            ]
-        else:
-            first, second = own_other, far
-            tags = far[CUT : CUT + 16, :].astype(F32)
-            charges = tags[0:1]
-            shifts = [tags[1 + p : 2 + p] for p in range(D2)]
-        across = jnp.broadcast_to(charges, (CHI, CHI))
-        gap = across - jnp.transpose(across)
-        for p in range(D2):
-            sums = slab(first, p) + slab(second, p).astype(F32)
-            ranged[which * CUT + p * CHI : which * CUT + (p + 1) * CHI, :] = jnp.where(
-                gap == shifts[p], sums, 0.0
-            )
-        gram = gram_of(ranged[which * CUT : (which + 1) * CUT, :])
-        diagonal = jnp.where(row == col, gram, 0.0)
-        mean = jnp.sum(jnp.sum(diagonal, axis=1, keepdims=True), axis=0, keepdims=True) / CHI
-        grams.append(gram + jnp.where(row == col, 0.01 * mean + 1e-06, 0.0))
-    inverses = eliminate(grams)
-    basis_own[...] = times_inverse(ranged[0:CUT, :], inverses[0]).astype(BF16)
-    basis_far[...] = times_inverse(ranged[CUT : 2 * CUT, :], inverses[1]).astype(BF16)
-    beside[...] = side_by_side(basis_own)
-    pack_rows(lambda p: slab(basis_far, p), wide, packed)
-    total[...] = jnp.zeros_like(total)
-
-    def consume(rows, block):
-        total[...] += dot_tn(packed[rows, :], block)
-
-    chain(natural, beside, layer, thin, consume)
-    result = unit(total[...])
+    tags = tagged[CUT : CUT + 16, :].astype(F32)
+    across = jnp.broadcast_to(tags[0:1], (CHI, CHI))
+    gap = across - jnp.transpose(across)
     for p in range(D2):
-        out_edge[p * CHI : (p + 1) * CHI, :] = result[:, p * CHI : (p + 1) * CHI]
-    out_own[...] = unit(corner_from(basis_own, pair_own))
-    far_corner = corner_from(basis_far, pair_far)
-    out_far[...] = unit(jnp.transpose(far_corner) if side else far_corner)
+        sums = slab(own, p) + slab(other, p).astype(F32)
+        ranged[p * CHI : (p + 1) * CHI, :] = jnp.where(gap == tags[1 + p : 2 + p], sums, 0.0)
+    gram = gram_of(ranged[...])
+    diagonal = jnp.where(row == col, gram, 0.0)
+    mean = jnp.sum(jnp.sum(diagonal, axis=1, keepdims=True), axis=0, keepdims=True) / CHI
+    return gram + jnp.where(row == col, 0.01 * mean + 1e-06, 0.0)
+
+
+def early_kernel(
+    from_lower, above_range, own_top, sent_top, beside,
+    above, top,
+    range_a, range_t,
+):
+    grams = [
+        range_and_gram(from_lower, above_range, above_range, range_a),
+        range_and_gram(own_top, beside, sent_top, range_t),
+    ]
+    inverses = []
+    run(eliminate(grams, inverses))
+    above[...] = times_inverse(range_a[...], inverses[0]).astype(BF16)
+    top[...] = times_inverse(range_t[...], inverses[1]).astype(BF16)
+
+
+def late_kernel(
+    own_left, sent_left, below, from_right, before_range, above, top,
+    left_rows, rows_t, lay_c, lay_a, corner_edge, corner_side, lower_pair, right_pair,
+    out_lu, out_le, out_ll, out_tl, out_te, out_tr,
+    range_l, range_b, left, before, beside_a, beside_t, mixed_l, mixed_t, packed, wide, thin_l, thin_t,
+):
+    grams = [
+        range_and_gram(own_left, below, sent_left, range_l),
+        range_and_gram(from_right, before_range, before_range, range_b),
+    ]
+
+    def keep_l(rows, block):
+        mixed_l[rows, :] = block
+
+    def keep_t(rows, block):
+        mixed_t[rows, :] = block
+
+    def products():
+        beside_t[...] = side_by_side(top)
+        yield from chain(rows_t, beside_t, lay_a, thin_t, keep_t)
+        beside_a[...] = side_by_side(above)
+        yield from chain(left_rows, beside_a, lay_c, thin_l, keep_l)
+        out_lu[...] = unit(corner_from(above, corner_edge))
+        out_tr[...] = unit(corner_from(top, right_pair))
+
+    inverses = []
+    weave(eliminate(grams, inverses), STEPS, products(), 2 * CHAIN_STEPS)
+    left[...] = times_inverse(range_l[...], inverses[0]).astype(BF16)
+    before[...] = times_inverse(range_b[...], inverses[1]).astype(BF16)
+    out_ll[...] = unit(corner_from(left, lower_pair))
+    out_tl[...] = unit(jnp.transpose(corner_from(before, corner_side)))
+    pack_rows(lambda p: slab(left, p), wide, packed)
+    result = unit(dot_tn(packed[...], mixed_l[...]))
+    for p in range(D2):
+        part = result[:, p * CHI : (p + 1) * CHI]
+        out_le[p * CHI : (p + 1) * CHI, :] = jnp.transpose(part)
+    pack_rows(lambda p: slab(before, p), wide, packed)
+    result = unit(dot_tn(packed[...], mixed_t[...]))
+    for p in range(D2):
+        out_te[p * CHI : (p + 1) * CHI, :] = result[:, p * CHI : (p + 1) * CHI]
 
 
 def shape(*dims, dtype=BF16):
     return jax.ShapeDtypeStruct(dims, dtype)
 
 
-def call(body, name, ins, outs, scratch, flops, far=()):
+def call(body, name, ins, outs, scratch, far=()):
     moved = sum(a.size * a.dtype.itemsize for a in ins) + sum(
         o.size * jnp.dtype(o.dtype).itemsize for o in outs
     )
@@ -452,8 +533,8 @@
         ],
         out_specs=(whole,) * len(outs),
         scratch_shapes=scratch,
-        compiler_params=pltpu.CompilerParams(vmem_limit_bytes=VMEM if name != "upper" else 60 * 1024 * 1024),
-        cost_estimate=pl.CostEstimate(flops=flops, bytes_accessed=moved, transcendentals=0),
+        compiler_params=pltpu.CompilerParams(vmem_limit_bytes=VMEM if name != "right" else 60 * 1024 * 1024),
+        cost_estimate=pl.CostEstimate(flops=1, bytes_accessed=1, transcendentals=0),
     )(*ins)
 
 
@@ -494,37 +575,40 @@
     virt_s = pltpu.SMEM((3, 1, 4), jnp.int32)
     env_v = keep(2, CHI, dtype=jnp.int32)
     arrivals = lambda n: pltpu.SemaphoreType.DMA((n,))
-    own_left, own_top, sent_left, sent_top, corner_edge, corner_side, lay_a, lay_b = call(
-        upper_kernel, "upper", [phys_charge, virt, site, env, ul, top, left, sketches],
-        [tall_wide, tall_wide, tagged, tagged, broad, broad, lay, lay],
-        [phys_s, virt_s, keep(27, 4, 3), env_v, keep(CHI, CHI), slabs, slabs, slabs, slabs, arrivals(9),
-         slabs, slabs, slabs, wide, thin, row_sum, keep(LAY, LAY), keep(216, CHI, dtype=F32)],
-        WORK[0], range(8),
-    )
+    from_right, sent_right, right_pair, rows_t, lay_a, lay_b, lay_c = call(
+        right_kernel, "right", [phys_charge, virt, site, ur, right, top, sketches],
+        [tall_wide, shape(CUT + 32, CHI), broad, tall, lay, lay, lay],
+        [phys_s, virt_s, keep(27, 4, 3), keep(CHI, CHI), slabs, slabs, slabs, arrivals(7), wide, thin,
+         keep(216, CHI, dtype=F32)],
+        range(7),
+    )
+    beside = from_behind(sent_right, "lx", -1)
+    own_left, own_top, sent_left, sent_top, corner_edge, corner_side, left_rows = call(
+        upper_kernel, "upper", [lay_c, virt, env, ul, top, left, sketches],
+        [tall_wide, tall_wide, tagged, tagged, broad, broad, tall],
+        [virt_s, env_v, keep(CHI, CHI), slabs, slabs, slabs, slabs, arrivals(7),
+         slabs, slabs, wide, thin, row_sum],
+        range(1, 7),
+    )
+    above_range = from_behind(sent_left, "ly", 1)
     before_range = from_behind(sent_top, "lx", 1)
-    above_range = from_behind(sent_left, "ly", 1)
-    others = [keep(CHI, CHI), slabs, slabs, slabs, arrivals(4), wide, thin]
-    from_lower, sent_lower, lower_pair, rows_l = call(
-        functools.partial(other_kernel, 1), "lower", [lay_b, ll, bottom, left, sketches],
-        [tall_wide, tall, broad, tall], others, WORK[1], range(1, 5),
+    from_lower, sent_lower, lower_pair = call(
+        lower_kernel, "lower", [lay_b, ll, bottom, left, sketches],
+        [tall_wide, tall, broad], [keep(CHI, CHI), slabs, slabs, slabs, arrivals(4), wide, thin, slabs],
+        range(1, 5),
     )
     below = from_behind(sent_lower, "ly", -1)
-    from_right, sent_right, right_pair, rows_t = call(
-        functools.partial(other_kernel, 3), "right", [lay_a, ur, right, top, sketches],
-        [tall_wide, tall, broad, tall], others, WORK[2], range(1, 5),
-    )
-    beside = from_behind(sent_right, "lx", -1)
-    bond = [virt_s, env_v, arrivals(2), keep(2 * CUT, CHI, dtype=F32), slabs, slabs,
-            keep(CHI, CUT), slabs, wide, thin, row_sum]
-    lo, le, lu = call(
-        functools.partial(bond_kernel, 0, 3), "left",
-        [virt, env, own_left, from_lower, below, above_range, rows_l, lay_b, lower_pair, corner_edge],
-        [corner, tall, corner], bond, WORK[3], range(2),
-    )
-    tr, te, tl = call(
-        functools.partial(bond_kernel, 1, 2), "top",
-        [virt, env, own_top, from_right, beside, before_range, rows_t, lay_a, right_pair, corner_side],
-        [corner, tall, corner], bond, WORK[4], range(2),
+    above, top_basis = call(
+        early_kernel, "early", [from_lower, above_range, own_top, sent_top, beside],
+        [tall, tall], [wide, wide],
+    )
+    square = keep(CUT, CUT)
+    lu, le, lo, tl, te, tr = call(
+        late_kernel, "late",
+        [own_left, sent_left, below, from_right, before_range, above, top_basis, left_rows, rows_t,
+         lay_c, lay_a, corner_edge, corner_side, lower_pair, right_pair],
+        [corner, tall, corner, corner, tall, corner],
+        [wide, wide, slabs, slabs, keep(CHI, CUT), keep(CHI, CUT), square, square, slabs, wide, thin, thin],
     )
     lift = lambda a: a[None, None]
     edge = lambda a: a.reshape(D2, CHI, CHI).transpose(1, 0, 2)[None, None]

time: 52.2 us -> 46.2 us (0.89)
  Pallas kernels: 38.3 us -> 29.1 us
  waiting for transfers between devices: 0.01 us -> 3.67 us
    pallas_call x5, Pallas kernels: 38.3 us -> 29.1 us  [call(): pl.pallas_call(body, name=name, out_shape=tuple(outs), in_specs=[pl.Block...]
    ppermute x4, waiting for transfers between devices: 0.01 us -> 3.67 us  [from_behind(): return lax.ppermute(block, axis, route)]
  transfers between devices with their start and end apart: 4 -> 4, of which waited for: 0 -> 1; matrix products, arithmetic and copies ran while one was open for 0% -> 0% of each run, Pallas kernels for 37% -> 30%
where the time goes in v3:
time: 46.2 us; the launch traced here: 46.1 us
  Pallas kernels  29.1 us (63%)
  starting transfers between devices  11.7 us (25%)
  waiting for transfers between devices  3.67 us (8%)
  between operations  0.9 us (2%)
  local copies, waits for them, and re-layouts  0.8 us (2%)
    pallas_call x5, Pallas kernels, call(): pl.pallas_call(body, name=name, out_shape=tuple(outs), in_specs=[pl.Block...  29.1 us
    ppermute x4, starting transfers between devices, from_behind(): return lax.ppermute(block, axis, route)  11.7 us
    ppermute x4, waiting for transfers between devices, from_behind(): return lax.ppermute(block, axis, route)  3.67 us
  transfers between devices with their start and end apart: 4, of which 1 were waited for; matrix products, arithmetic and copies ran while one was open for 0% of the time, Pallas kernels for 30%

profile of v3, /device:TPU:8, one launch (start us, length us, event | category | flops | bytes accessed | tf_op | source)
XLA Modules:
  0.0 46.1 jit_solution(17968985594066693171)
XLA Ops:
  0.6 0.0 copy-start
  0.6 0.0 copy-start.1
  0.7 5.4 %right.1 = (f32[1152,128]{1,0:T(8,128)}, bf16[1184,128]{1,0:T(8,128)(2,1)}, bf16[128,1152]{1,0:T(8,128)(2,1)}, bf16[1152,128]{1,0:T(8,128)(2,1)}, bf16[96,96]{1,...) custom-call(s32[1,1,4]{2,1,0:T(1,128)} %phys_h.1, s32[3,1,4]{2,1,0:T(1,128)} %bitcast.55, ...), custom_call_target="tpu_custom_call" | custom-call | flops 1 | bytes 1 | tf_op jit(solution)/shard_map/right/pallas_call | solution.py:527
  6.1 0.0 copy-start.6
  6.1 7.7 %collective-permute-start.3 = (bf16[1184,128]{1,0:T(8,128)(2,1)}, bf16[1184,128]{1,0:T(8,128)(2,1)S(1)}, u32[]{:S(2)}, u32[]{:S(2)}) collective-permute-start(bf16[1184,128]{1,0:T(8,128)(2,1)} %get-tuple-element.40), channel_id=1, source_target_pairs={{16,0},{32,16},{48,32},{64,48},{80,64},{96,80},{112,96},{128,112},... | collective-permute-start | bytes 909320 | tf_op jit(solution)/shard_map/ppermute | solution.py:544
  13.8 0.0 copy-done
  13.8 0.0 copy-done.13
  13.8 0.0 copy-start.7
  13.8 0.7 %copy-done.7 = bf16[96,96]{1,0:T(8,128)(2,1)S(1)} copy-done((bf16[96,96]{1,0:T(8,128)(2,1)S(1)}, bf16[96,96]{1,0:T(8,128)(2,1)}, u32[]{:S(2)}) %copy-start.7) | copy-done | bytes 18456
  14.6 4.4 %upper.1 = (f32[1152,128]{1,0:T(8,128)S(1)}, f32[1152,128]{1,0:T(8,128)S(1)}, bf16[1168,128]{1,0:T(8,128)(2,1)S(1)}, bf16[1168,128]{1,0:T(8,128)(2,1)S(1)}, bf16...) custom-call(bf16[96,96]{1,0:T(8,128)(2,1)S(1)} %copy-done.7, ...), custom_call_target="tpu_custom_call" | custom-call | flops 1 | bytes 1 | tf_op jit(solution)/shard_map/upper/pallas_call | solution.py:527
  19.0 0.1 collective-permute-start.2
  19.1 0.3 collective-permute-start.1
  19.4 3.3 %lower.1 = (f32[1152,128]{1,0:T(8,128)S(1)}, bf16[1152,128]{1,0:T(8,128)(2,1)S(1)}, bf16[128,1152]{1,0:T(8,128)(2,1)S(1)}) custom-call(bf16[96,96]{1,0:T(8,128)(2,1)S(1)} %copy-done.12, bf16[128,128]{1,0:T(8,128)(2,1)S(1)} %bitcast.54, bf16[1152,128]{1,0:T(8,128)(2,1)S(1)} %bitcast.52, bf16[1152,128]{1,0:T(8,128)(2,1)S(1)} %bitcast.51, ...), custom_call_target="tpu_custom_call" | custom-call | flops 1 | bytes 1 | tf_op jit(solution)/shard_map/lower/pallas_call | solution.py:527
  22.7 0.0 copy-start.4
  22.7 0.0 copy-start.5
  22.7 0.0 copy-start.8
  22.7 0.0 copy-start.11
  22.7 3.7 %collective-permute-start = (bf16[1152,128]{1,0:T(8,128)(2,1)S(1)}, bf16[1152,128]{1,0:T(8,128)(2,1)S(1)}, u32[]{:S(2)}, u32[]{:S(2)}) collective-permute-start(bf16[1152,128]{1,0:T(8,128)(2,1)S(1)} %get-tuple-element.35), channel_id=1, source_target_pairs={{1,0},{2,1},{3,2},{4,3},{5,4},{6,5},{7,6},{8,7},{9,8},{10,9},{11,1... | collective-permute-start | bytes 884744 | tf_op jit(solution)/shard_map/ppermute | solution.py:544
  26.4 3.7 %collective-permute-done.2.above_range = bf16[1168,128]{1,0:T(8,128)(2,1)S(1)} collective-permute-done((bf16[1168,128]{1,0:T(8,128)(2,1)S(1)}, bf16[1168,128]{1,0:T(8,128)(2,1)S(1)}, u32[]{:S(2)}, u32[]{:S(2)}) %collective-permute-start.2) | collective-permute-done | bytes 299040 | tf_op jit(solution)/shard_map/ppermute | solution.py:544
  30.0 0.0 collective-permute-done.3.beside
  30.0 6.4 %early.1 = (bf16[1152,128]{1,0:T(8,128)(2,1)S(1)}, bf16[1152,128]{1,0:T(8,128)(2,1)S(1)}) custom-call(f32[1152,128]{1,0:T(8,128)S(1)} %get-tuple-element.38.from_lower, bf16[1168,128]{1,0:T(8,128)(2,1)S(1)} %collective-permute-done.2.above_range, f32[1152,128]{1,0:T(8,128)S(1)} %get-tuple-element.39.own_top, ...), custom_call_target="tpu_custom_call" | custom-call | flops 1 | bytes 1 | tf_op jit(solution)/shard_map/early/pallas_call | solution.py:527
  36.4 0.0 collective-permute-done.below
  36.4 0.0 collective-permute-done.1.before_range
  36.5 9.6 %late.1 = (bf16[128,128]{1,0:T(8,128)(2,1)}, bf16[1152,128]{1,0:T(8,128)(2,1)}, bf16[128,128]{1,0:T(8,128)(2,1)}, bf16[128,128]{1,0:T(8,128)(2,1)}, bf16[1152,128]{1,0:T(8,128)(2,1)}, /*index=5*/bf16[128,128]{1,0:T(8,128)(2,1)}) custom-call(f32[1152,128]{1,0:T(8,128)S(1)} %get-tuple-element.32.own_left, bf16[1168,128]{1,0:T(8,128)(2,1)S(1)} %get-tuple-element.33.sent_left, ...), custom_call_target="tpu_custom_call" | custom-call | flops 1 | bytes 1 | tf_op jit(solution)/shard_map/late/pallas_call | solution.py:527
  (19 shorter events, 0.0 us)
Async XLA Ops:
  0.6 13.2 %copy-start = (bf16[1,1,4,1152,128]{4,3,2,1,0:T(8,128)(2,1)S(1)}, bf16[1,1,4,1152,128]{4,3,2,1,0:T(8,128)(2,1)}, u32[]{:S(2)}) copy-start(bf16[1,1,4,1152,128]{4,3,2,1,0:T(8,128)(2,1)} %param.23) | copy-start | bytes 3538948
  0.6 13.2 %copy-start.1 = (bf16[1,1,128,9,128]{4,2,3,1,0:T(8,128)(2,1)S(1)}, bf16[1,1,128,9,128]{4,2,3,1,0:T(8,128)(2,1)}, u32[]{:S(2)}) copy-start(bf16[1,1,128,9,128]{4,2,3,1,0:T(8,128)(2,1)} %param.19) | copy-start | bytes 884740
  0.7 13.2 %copy-start.13 = (s32[1,1,4,3]{2,1,3,0:T(1,128)S(1)}, s32[1,1,4,3]{2,1,3,0:T(1,128)}, u32[]{:S(2)}) copy-start(s32[1,1,4,3]{2,1,3,0:T(1,128)} %param.14) | copy-start | bytes 148
  0.7 13.1 %copy-start.2 = (bf16[1,1,128,9,128]{4,2,3,1,0:T(8,128)(2,1)S(1)}, bf16[1,1,128,9,128]{4,2,3,1,0:T(8,128)(2,1)}, u32[]{:S(2)}) copy-start(bf16[1,1,128,9,128]{4,2,3,1,0:T(8,128)(2,1)} %param.22) | copy-start | bytes 884740
  0.7 13.1 %copy-start.9 = (bf16[1,1,128,128]{3,2,1,0:T(8,128)(2,1)S(1)}, bf16[1,1,128,128]{3,2,1,0:T(8,128)(2,1)}, u32[]{:S(2)}) copy-start(bf16[1,1,128,128]{3,2,1,0:T(8,128)(2,1)} %param.16) | copy-start | bytes 98308
  0.7 13.1 %copy-start.14 = (s32[1,1,2,128]{3,2,1,0:T(2,128)S(1)}, s32[1,1,2,128]{3,2,1,0:T(2,128)}, u32[]{:S(2)}) copy-start(s32[1,1,2,128]{3,2,1,0:T(2,128)} %param.15) | copy-start | bytes 3076
  0.7 18.6 %copy-start.10 = (bf16[1,1,128,128]{3,2,1,0:T(8,128)(2,1)S(1)}, bf16[1,1,128,128]{3,2,1,0:T(8,128)(2,1)}, u32[]{:S(2)}) copy-start(bf16[1,1,128,128]{3,2,1,0:T(8,128)(2,1)} %param.18) | copy-start | bytes 98308
  6.1 13.2 %copy-start.6 = (bf16[1,1,128,9,128]{4,2,3,1,0:T(8,128)(2,1)S(1)}, bf16[1,1,128,9,128]{4,2,3,1,0:T(8,128)(2,1)}, u32[]{:S(2)}) copy-start(bf16[1,1,128,9,128]{4,2,3,1,0:T(8,128)(2,1)} %param.21) | copy-start | bytes 884740
  6.1 23.9 %collective-permute-start.3 = (bf16[1184,128]{1,0:T(8,128)(2,1)}, bf16[1184,128]{1,0:T(8,128)(2,1)S(1)}, u32[]{:S(2)}, u32[]{:S(2)}) collective-permute-start(bf16[1184,128]{1,0:T(8,128)(2,1)} %get-tuple-element.40), channel_id=1, source_target_pairs={{16,0},{32,16},{48,32},{64,48},{80,64},{96,80},{112,96},{128,112},... | collective-permute-start | bytes 909320 | tf_op jit(solution)/shard_map/ppermute | solution.py:544
  13.8 0.7 %copy-start.7 = (bf16[96,96]{1,0:T(8,128)(2,1)S(1)}, bf16[96,96]{1,0:T(8,128)(2,1)}, u32[]{:S(2)}) copy-start(bf16[96,96]{1,0:T(8,128)(2,1)} %get-tuple-element.31.lay_c) | copy-start | bytes 55300
  14.6 4.8 %copy-start.12 = (bf16[96,96]{1,0:T(8,128)(2,1)S(1)}, bf16[96,96]{1,0:T(8,128)(2,1)}, u32[]{:S(2)}) copy-start(bf16[96,96]{1,0:T(8,128)(2,1)} %get-tuple-element.34.layer) | copy-start | bytes 55300
  19.0 11.1 %collective-permute-start.2 = (bf16[1168,128]{1,0:T(8,128)(2,1)S(1)}, bf16[1168,128]{1,0:T(8,128)(2,1)S(1)}, u32[]{:S(2)}, u32[]{:S(2)}) collective-permute-start(bf16[1168,128]{1,0:T(8,128)(2,1)S(1)} %get-tuple-element.33.sent_left), channel_id=1, source_target_pairs={{15,0},{0,1},{1,2},{2,3},{3,4},{4,5},{5,6},{6,7},{7,8},{8,9},{9,10... | collective-permute-start | bytes 897032 | tf_op jit(solution)/shard_map/ppermute | solution.py:544
  19.1 17.4 %collective-permute-start.1 = (bf16[1168,128]{1,0:T(8,128)(2,1)S(1)}, bf16[1168,128]{1,0:T(8,128)(2,1)S(1)}, u32[]{:S(2)}, u32[]{:S(2)}) collective-permute-start(bf16[1168,128]{1,0:T(8,128)(2,1)S(1)} %get-tuple-element.37.sent_top), channel_id=1, source_target_pairs={{240,0},{0,16},{16,32},{32,48},{48,64},{64,80},{80,96},{96,112},{1... | collective-permute-start | bytes 897032 | tf_op jit(solution)/shard_map/ppermute | solution.py:544
  22.7 13.8 %copy-start.3 = (f32[1152,128]{1,0:T(8,128)S(1)}, f32[1152,128]{1,0:T(8,128)}, u32[]{:S(2)}) copy-start(f32[1152,128]{1,0:T(8,128)} %get-tuple-element.36.from_right) | copy-start | bytes 1769476
  22.7 13.8 %copy-start.4 = (bf16[128,1152]{1,0:T(8,128)(2,1)S(1)}, bf16[128,1152]{1,0:T(8,128)(2,1)}, u32[]{:S(2)}) copy-start(bf16[128,1152]{1,0:T(8,128)(2,1)} %get-tuple-element.49.right_pair) | copy-start | bytes 884740
  22.7 13.8 %copy-start.5 = (bf16[1152,128]{1,0:T(8,128)(2,1)S(1)}, bf16[1152,128]{1,0:T(8,128)(2,1)}, u32[]{:S(2)}) copy-start(bf16[1152,128]{1,0:T(8,128)(2,1)} %get-tuple-element.44.rows_t) | copy-start | bytes 884740
  22.7 13.8 %copy-start.8 = (bf16[96,96]{1,0:T(8,128)(2,1)S(1)}, bf16[96,96]{1,0:T(8,128)(2,1)}, u32[]{:S(2)}) copy-start(bf16[96,96]{1,0:T(8,128)(2,1)} %get-tuple-element.31.lay_c) | copy-start | bytes 55300
  22.7 13.8 %copy-start.11 = (bf16[96,96]{1,0:T(8,128)(2,1)S(1)}, bf16[96,96]{1,0:T(8,128)(2,1)}, u32[]{:S(2)}) copy-start(bf16[96,96]{1,0:T(8,128)(2,1)} %get-tuple-element.45.lay_a) | copy-start | bytes 55300
  22.7 13.7 %collective-permute-start = (bf16[1152,128]{1,0:T(8,128)(2,1)S(1)}, bf16[1152,128]{1,0:T(8,128)(2,1)S(1)}, u32[]{:S(2)}, u32[]{:S(2)}) collective-permute-start(bf16[1152,128]{1,0:T(8,128)(2,1)S(1)} %get-tuple-element.35), channel_id=1, source_target_pairs={{1,0},{2,1},{3,2},{4,3},{5,4},{6,5},{7,6},{8,7},{9,8},{10,9},{11,1... | collective-permute-start | bytes 884744 | tf_op jit(solution)/shard_map/ppermute | solution.py:544

commit v4 on v3

--- a/solution.py
+++ b/solution.py
@@ -193,23 +193,21 @@
     return jnp.where(total == 0, rows, 0.0)
 
 
-def build_layers(kept, out_a, out_b, out_c):
-    m_ru, m_dl, m_rd, m_ul = layer_masks()
-
-    def build(rows, cols):
-        halves = []
+def build_layers(kept, *wanted):
+    masks = dict(zip(("ru", "dl", "rd", "ul"), layer_masks()))
+
+    for out, rows, cols in wanted:
+        halves_of = []
         for half in range(2):
-            tall = jnp.concatenate([rows[half] * kept[s : s + 1, :] for s in range(4)], axis=0)
-            halves.append(dot_nt(tall.astype(BF16), cols[half].astype(BF16)))
-        ket_bra = halves[0] * halves[1]
+            tall = jnp.concatenate(
+                [masks[rows][half] * kept[s : s + 1, :] for s in range(4)], axis=0
+            )
+            halves_of.append(dot_nt(tall.astype(BF16), masks[cols][half].astype(BF16)))
+        ket_bra = halves_of[0] * halves_of[1]
         total = ket_bra[:LAY]
         for s in range(1, 4):
             total = total + ket_bra[s * LAY : (s + 1) * LAY]
-        return total.astype(BF16)
-
-    out_a[...] = build(m_dl, m_ru)
-    out_b[...] = build(m_ru, m_dl)
-    out_c[...] = build(m_rd, m_ul)
+        out[...] = total.astype(BF16)
 
 
 def unpack_term(wide, term, sent):
@@ -243,7 +241,7 @@
 
 def right_kernel(
     phys_h, virt_h, site_h, corner_h, edge_h, edge_rows_h, sketches,
-    term, sent, pair_out, rows_out, lay_a, lay_b, lay_c,
+    term, sent, pair_out, rows_out, lay_a, lay_b,
     phys, virt, site, corner, edge, edge_rows, sketch, arrived, wide, thin, small,
 ):
     copies = bring(
@@ -253,9 +251,12 @@
     )
     for copy in copies[:3]:
         copy.wait()
-    build_layers(kept_rows(site, phys, virt, small), lay_a, lay_b, lay_c)
+    kept = kept_rows(site, phys, virt, small)
+    for copy in copies[3:]:
+        copy.wait()
+    build_layers(kept, (lay_a, "dl", "ru"), (lay_b, "ru", "dl"))
     sent[CUT : CUT + 32, :] = jnp.zeros((32, CHI), BF16)
-    corner_product(copies[3:], corner, edge, edge_rows, sketch, lay_a, term, sent, pair_out, rows_out, wide, thin)
+    corner_product((), corner, edge, edge_rows, sketch, lay_a, term, sent, pair_out, rows_out, wide, thin)
 
 
 def lower_kernel(
@@ -274,11 +275,12 @@
 def corner_product(
     copies, corner, edge, edge_rows, sketch, layer, term, sent, pair_out, rows_out, wide, thin
 ):
-    for copy in copies[:3]:
+    for copy in copies[:2]:
         copy.wait()
     pair_out[...] = dot(corner[...], side_by_side(edge)).astype(BF16)
+    for copy in copies[2:]:
+        copy.wait()
     pack_rows(lambda p: slab(edge_rows, p), wide, rows_out)
-    copies[3].wait()
 
     def consume(rows, block):
         wide[rows, :] = dot(block, sketch[...])
@@ -288,35 +290,35 @@
 
 
 def upper_kernel(
-    lay_c, virt_h, env_h, corner_h, edge_t_h, edge_l_h, sketches,
-    own_left, own_top, sent_left, sent_top, corner_edge, corner_side, left_rows,
-    virt, env, corner, edge_t, edge_l, sketch_l, sketch_t, arrived,
-    sketch_cols, sketch_rows, wide, thin, top_sum,
+    phys_h, virt_h, site_h, env_h, corner_h, edge_t_h, edge_l_h, sketches,
+    own_left, own_top, sent_left, sent_top, corner_edge, corner_side, left_rows, lay_c,
+    phys, virt, site, env, corner, edge_t, edge_l, sketch_l, sketch_t, arrived,
+    sketch_cols, sketch_rows, wide, thin, top_sum, small,
 ):
     first = sketches.at[pl.ds(0, CUT), :]
     third_one = sketches.at[pl.ds(2 * CUT, CUT), :]
     copies = bring(
-        (virt_h, env_h, corner_h, edge_t_h, edge_l_h, first, third_one),
-        (virt, env, corner, edge_t, edge_l, sketch_l, sketch_t),
+        (corner_h, edge_t_h, edge_l_h, phys_h, virt_h, site_h, env_h, first, third_one),
+        (corner, edge_t, edge_l, phys, virt, site, env, sketch_l, sketch_t),
         arrived,
     )
-    for copy in copies[:5]:
+    top_sum[...] = jnp.zeros_like(top_sum)
+    for copy in copies:
         copy.wait()
+    kept = kept_rows(site, phys, virt, small)
     charges = env[...].astype(F32)
     add_charges(sent_left, charges[0:1], virt, 3)
     add_charges(sent_top, charges[1:2], virt, 2)
     corner_edge[...] = dot(corner[...], side_by_side(edge_t)).astype(BF16)
     corner_side[...] = dot_tn(corner[...], side_by_side(edge_l)).astype(BF16)
+    build_layers(kept, (lay_c, "rd", "ul"))
     pack_rows(lambda p: jnp.transpose(slab(edge_l, p).astype(F32)), wide, left_rows)
-    copies[5].wait()
     wide[...] = sketch_l[...].astype(F32)
     for p in range(D2):
         sketch_cols[p * CHI : (p + 1) * CHI, :] = wide[pl.ds(p, CHI, stride=D2), :].astype(BF16)
-    copies[6].wait()
     wide[...] = sketch_t[...].astype(F32)
     picked = [wide[pl.ds(p, CHI, stride=D2), :] for p in range(D2)]
     pack_rows(lambda p: picked[p], wide, sketch_rows)
-    top_sum[...] = jnp.zeros_like(top_sum)
 
     def consume(rows, block):
         wide[rows, :] = dot(block, sketch_cols[...])
@@ -419,14 +421,23 @@
 
 def gram_of(ranged):
     high, low = halves(ranged)
-    cross = dot_tn(high, low)
-    return dot_tn(high, high) + (cross + jnp.transpose(cross))
+    both = dot_tn(high, jnp.concatenate([high, low], axis=1))
+    cross = both[:, CHI:]
+    return both[:, :CHI] + (cross + jnp.transpose(cross))
 
 
 def times_inverse(ranged, inverse):
     high, low = halves(ranged)
     inv_high, inv_low = halves(inverse)
-    return dot_nt(high, inv_high) + (dot_nt(high, inv_low) + dot_nt(low, inv_high))
+    factors = jnp.concatenate(
+        [
+            jnp.concatenate([inv_high, inv_high], axis=1),
+            jnp.concatenate([inv_low, jnp.zeros_like(inv_low)], axis=1),
+        ],
+        axis=0,
+    )
+    both = dot_nt(jnp.concatenate([high, low], axis=1), factors)
+    return both[:, :CHI] + both[:, CHI:]
 
 
 def unit(values):
@@ -575,20 +586,20 @@
     virt_s = pltpu.SMEM((3, 1, 4), jnp.int32)
     env_v = keep(2, CHI, dtype=jnp.int32)
     arrivals = lambda n: pltpu.SemaphoreType.DMA((n,))
-    from_right, sent_right, right_pair, rows_t, lay_a, lay_b, lay_c = call(
+    from_right, sent_right, right_pair, rows_t, lay_a, lay_b = call(
         right_kernel, "right", [phys_charge, virt, site, ur, right, top, sketches],
-        [tall_wide, shape(CUT + 32, CHI), broad, tall, lay, lay, lay],
+        [tall_wide, shape(CUT + 32, CHI), broad, tall, lay, lay],
         [phys_s, virt_s, keep(27, 4, 3), keep(CHI, CHI), slabs, slabs, slabs, arrivals(7), wide, thin,
          keep(216, CHI, dtype=F32)],
         range(7),
     )
     beside = from_behind(sent_right, "lx", -1)
-    own_left, own_top, sent_left, sent_top, corner_edge, corner_side, left_rows = call(
-        upper_kernel, "upper", [lay_c, virt, env, ul, top, left, sketches],
-        [tall_wide, tall_wide, tagged, tagged, broad, broad, tall],
-        [virt_s, env_v, keep(CHI, CHI), slabs, slabs, slabs, slabs, arrivals(7),
-         slabs, slabs, wide, thin, row_sum],
-        range(1, 7),
+    own_left, own_top, sent_left, sent_top, corner_edge, corner_side, left_rows, lay_c = call(
+        upper_kernel, "upper", [phys_charge, virt, site, env, ul, top, left, sketches],
+        [tall_wide, tall_wide, tagged, tagged, broad, broad, tall, lay],
+        [phys_s, virt_s, keep(27, 4, 3), env_v, keep(CHI, CHI), slabs, slabs, slabs, slabs, arrivals(9),
+         slabs, slabs, wide, thin, row_sum, keep(216, CHI, dtype=F32)],
+        range(8),
     )
     above_range = from_behind(sent_left, "ly", 1)
     before_range = from_behind(sent_top, "lx", 1)

time: 46.2 us -> 45.4 us (0.983)
  local copies, waits for them, and re-layouts: 0.8 us -> 0.08 us
    unnamed x30, local copies, waits for them, and re-layouts: 0.8 us -> 0.08 us
  transfers between devices with their start and end apart: 4 -> 4, of which waited for: 1 -> 1; matrix products, arithmetic and copies ran while one was open for 0% -> 0% of each run, Pallas kernels for 30% -> 31%
where the time goes in v4:
time: 45.4 us; the launch traced here: 45.2 us
  Pallas kernels  28.8 us (63%)
  starting transfers between devices  11.6 us (26%)
  waiting for transfers between devices  3.78 us (8%)
  between operations  0.91 us (2%)
    pallas_call x5, Pallas kernels, call(): pl.pallas_call(body, name=name, out_shape=tuple(outs), in_specs=[pl.Block...  28.8 us
    ppermute x4, starting transfers between devices, from_behind(): return lax.ppermute(block, axis, route)  11.6 us
    ppermute x4, waiting for transfers between devices, from_behind(): return lax.ppermute(block, axis, route)  3.78 us
  transfers between devices with their start and end apart: 4, of which 1 were waited for; matrix products, arithmetic and copies ran while one was open for 0% of the time, Pallas kernels for 31%

profile of v4, /device:TPU:8, one launch (start us, length us, event | category | flops | bytes accessed | tf_op | source)
XLA Modules:
  0.0 45.2 jit_solution(16533430579760664574)
XLA Ops:
  0.7 5.4 %right.1 = (f32[1152,128]{1,0:T(8,128)}, bf16[1184,128]{1,0:T(8,128)(2,1)}, bf16[128,1152]{1,0:T(8,128)(2,1)}, bf16[1152,128]{1,0:T(8,128)(2,1)}, bf16[96,96]{1,0:T(8,128)(2,1)}, /*index=5*/bf16[96,96]{1,0:T(8,128)(2,1)}) custom-call(s32[1,1,4]{2,1,0:T(1,128)} %phys_h.3, s32[3,1,4]{2,1,0:T(1,128)} %bitcast.57, bf16[27,4,3]{2,1,0:T(4,128)(2,1)} %bitcast.53, ...), custom_call_target="tpu_custom_call" | custom-call | flops 1 | bytes 1 | tf_op jit(solution)/shard_map/right/pallas_call | solution.py:538
  6.1 0.0 copy-start.6
  6.1 0.0 copy-start.9
  6.1 0.0 copy-start.11
  6.1 7.7 %collective-permute-start.3 = (bf16[1184,128]{1,0:T(8,128)(2,1)}, bf16[1184,128]{1,0:T(8,128)(2,1)S(1)}, u32[]{:S(2)}, u32[]{:S(2)}) collective-permute-start(bf16[1184,128]{1,0:T(8,128)(2,1)} %get-tuple-element.39), channel_id=1, source_target_pairs={{16,0},{32,16},{48,32},{64,48},{80,64},{96,80},{112,96},{128,112},... | collective-permute-start | bytes 909320 | tf_op jit(solution)/shard_map/ppermute | solution.py:555
  13.8 0.0 copy-done.13
  13.8 0.0 copy-done.7
  13.8 0.0 copy-done.2
  13.8 0.0 copy-done.8
  13.8 0.0 copy-done.14
  13.8 4.6 %upper.1 = (f32[1152,128]{1,0:T(8,128)S(1)}, f32[1152,128]{1,0:T(8,128)S(1)}, bf16[1168,128]{1,0:T(8,128)(2,1)S(1)}, bf16[1168,128]{1,0:T(8,128)(2,1)S(1)}, bf16...) custom-call(s32[1,1,4]{2,1,0:T(1,128)S(1)} %copy-done.13, ...), custom_call_target="tpu_custom_call" | custom-call | flops 1 | bytes 1 | tf_op jit(solution)/shard_map/upper/pallas_call | solution.py:538
  18.4 0.1 collective-permute-start.2
  18.5 0.3 collective-permute-start.1
  18.8 3.2 %lower.1 = (f32[1152,128]{1,0:T(8,128)S(1)}, bf16[1152,128]{1,0:T(8,128)(2,1)S(1)}, bf16[128,1152]{1,0:T(8,128)(2,1)S(1)}) custom-call(bf16[96,96]{1,0:T(8,128)(2,1)S(1)} %copy-done.11, bf16[128,128]{1,0:T(8,128)(2,1)S(1)} %bitcast.56, bf16[1152,128]{1,0:T(8,128)(2,1)S(1)} %bitcast.52, bf16[1152,128]{1,0:T(8,128)(2,1)S(1)} %bitcast.51, ...), custom_call_target="tpu_custom_call" | custom-call | flops 1 | bytes 1 | tf_op jit(solution)/shard_map/lower/pallas_call | solution.py:538
  22.1 0.0 copy-start.4
  22.1 0.0 copy-start.5
  22.1 0.0 copy-start.10
  22.1 3.6 %collective-permute-start = (bf16[1152,128]{1,0:T(8,128)(2,1)S(1)}, bf16[1152,128]{1,0:T(8,128)(2,1)S(1)}, u32[]{:S(2)}, u32[]{:S(2)}) collective-permute-start(bf16[1152,128]{1,0:T(8,128)(2,1)S(1)} %get-tuple-element.34), channel_id=1, source_target_pairs={{1,0},{2,1},{3,2},{4,3},{5,4},{6,5},{7,6},{8,7},{9,8},{10,9},{11,1... | collective-permute-start | bytes 884744 | tf_op jit(solution)/shard_map/ppermute | solution.py:555
  25.7 3.8 %collective-permute-done.2.above_range = bf16[1168,128]{1,0:T(8,128)(2,1)S(1)} collective-permute-done((bf16[1168,128]{1,0:T(8,128)(2,1)S(1)}, bf16[1168,128]{1,0:T(8,128)(2,1)S(1)}, u32[]{:S(2)}, u32[]{:S(2)}) %collective-permute-start.2) | collective-permute-done | bytes 299040 | tf_op jit(solution)/shard_map/ppermute | solution.py:555
  29.5 0.0 collective-permute-done.3.beside
  29.5 6.2 %early.1 = (bf16[1152,128]{1,0:T(8,128)(2,1)S(1)}, bf16[1152,128]{1,0:T(8,128)(2,1)S(1)}) custom-call(f32[1152,128]{1,0:T(8,128)S(1)} %get-tuple-element.37.from_lower, bf16[1168,128]{1,0:T(8,128)(2,1)S(1)} %collective-permute-done.2.above_range, f32[1152,128]{1,0:T(8,128)S(1)} %get-tuple-element.38.own_top, ...), custom_call_target="tpu_custom_call" | custom-call | flops 1 | bytes 1 | tf_op jit(solution)/shard_map/early/pallas_call | solution.py:538
  35.8 0.0 collective-permute-done.below
  35.8 0.0 collective-permute-done.1.before_range
  35.8 9.4 %late.1 = (bf16[128,128]{1,0:T(8,128)(2,1)}, bf16[1152,128]{1,0:T(8,128)(2,1)}, bf16[128,128]{1,0:T(8,128)(2,1)}, bf16[128,128]{1,0:T(8,128)(2,1)}, bf16[1152,128]{1,0:T(8,128)(2,1)}, /*index=5*/bf16[128,128]{1,0:T(8,128)(2,1)}) custom-call(f32[1152,128]{1,0:T(8,128)S(1)} %get-tuple-element.31.own_left, bf16[1168,128]{1,0:T(8,128)(2,1)S(1)} %get-tuple-element.32.sent_left, ...), custom_call_target="tpu_custom_call" | custom-call | flops 1 | bytes 1 | tf_op jit(solution)/shard_map/late/pallas_call | solution.py:538
  (19 shorter events, 0.0 us)
Async XLA Ops:
  0.6 13.2 %copy-start.13 = (s32[1,1,4]{2,1,0:T(1,128)S(1)}, s32[1,1,4]{2,1,0:T(1,128)}, u32[]{:S(2)}) copy-start(s32[1,1,4]{2,1,0:T(1,128)} %phys_h.3) | copy-start | bytes 52
  0.6 13.1 %copy-start = (bf16[1,1,4,1152,128]{4,3,2,1,0:T(8,128)(2,1)S(1)}, bf16[1,1,4,1152,128]{4,3,2,1,0:T(8,128)(2,1)}, u32[]{:S(2)}) copy-start(bf16[1,1,4,1152,128]{4,3,2,1,0:T(8,128)(2,1)} %param.23) | copy-start | bytes 3538948
  0.7 13.1 %copy-start.1 = (bf16[1,1,128,9,128]{4,2,3,1,0:T(8,128)(2,1)S(1)}, bf16[1,1,128,9,128]{4,2,3,1,0:T(8,128)(2,1)}, u32[]{:S(2)}) copy-start(bf16[1,1,128,9,128]{4,2,3,1,0:T(8,128)(2,1)} %param.19) | copy-start | bytes 884740
  0.7 13.1 %copy-start.12 = (s32[1,1,4,3]{2,1,3,0:T(1,128)S(1)}, s32[1,1,4,3]{2,1,3,0:T(1,128)}, u32[]{:S(2)}) copy-start(s32[1,1,4,3]{2,1,3,0:T(1,128)} %param.14) | copy-start | bytes 148
  0.7 13.1 %copy-start.7 = (bf16[1,1,4,3,3,3,3]{6,2,5,4,3,1,0:T(4,128)(2,1)S(1)}, bf16[1,1,4,3,3,3,3]{6,2,5,4,3,1,0:T(4,128)(2,1)}, u32[]{:S(2)}) copy-start(bf16[1,1,4,3,3,3,3]{6,2,5,4,3,1,0:T(4,128)(2,1)} %param.12) | copy-start | bytes 1948
  0.7 13.1 %copy-start.2 = (bf16[1,1,128,9,128]{4,2,3,1,0:T(8,128)(2,1)S(1)}, bf16[1,1,128,9,128]{4,2,3,1,0:T(8,128)(2,1)}, u32[]{:S(2)}) copy-start(bf16[1,1,128,9,128]{4,2,3,1,0:T(8,128)(2,1)} %param.22) | copy-start | bytes 884740
  0.7 13.1 %copy-start.8 = (bf16[1,1,128,128]{3,2,1,0:T(8,128)(2,1)S(1)}, bf16[1,1,128,128]{3,2,1,0:T(8,128)(2,1)}, u32[]{:S(2)}) copy-start(bf16[1,1,128,128]{3,2,1,0:T(8,128)(2,1)} %param.16) | copy-start | bytes 98308
  0.7 13.1 %copy-start.14 = (s32[1,1,2,128]{3,2,1,0:T(2,128)S(1)}, s32[1,1,2,128]{3,2,1,0:T(2,128)}, u32[]{:S(2)}) copy-start(s32[1,1,2,128]{3,2,1,0:T(2,128)} %param.15) | copy-start | bytes 3076
  6.1 12.7 %copy-start.6 = (bf16[1,1,128,9,128]{4,2,3,1,0:T(8,128)(2,1)S(1)}, bf16[1,1,128,9,128]{4,2,3,1,0:T(8,128)(2,1)}, u32[]{:S(2)}) copy-start(bf16[1,1,128,9,128]{4,2,3,1,0:T(8,128)(2,1)} %param.21) | copy-start | bytes 884740
  6.1 12.7 %copy-start.9 = (bf16[1,1,128,128]{3,2,1,0:T(8,128)(2,1)S(1)}, bf16[1,1,128,128]{3,2,1,0:T(8,128)(2,1)}, u32[]{:S(2)}) copy-start(bf16[1,1,128,128]{3,2,1,0:T(8,128)(2,1)} %param.18) | copy-start | bytes 98308
  6.1 12.7 %copy-start.11 = (bf16[96,96]{1,0:T(8,128)(2,1)S(1)}, bf16[96,96]{1,0:T(8,128)(2,1)}, u32[]{:S(2)}) copy-start(bf16[96,96]{1,0:T(8,128)(2,1)} %get-tuple-element.33.layer) | copy-start | bytes 55300
  6.1 23.4 %collective-permute-start.3 = (bf16[1184,128]{1,0:T(8,128)(2,1)}, bf16[1184,128]{1,0:T(8,128)(2,1)S(1)}, u32[]{:S(2)}, u32[]{:S(2)}) collective-permute-start(bf16[1184,128]{1,0:T(8,128)(2,1)} %get-tuple-element.39), channel_id=1, source_target_pairs={{16,0},{32,16},{48,32},{64,48},{80,64},{96,80},{112,96},{128,112},... | collective-permute-start | bytes 909320 | tf_op jit(solution)/shard_map/ppermute | solution.py:555
  18.4 11.1 %collective-permute-start.2 = (bf16[1168,128]{1,0:T(8,128)(2,1)S(1)}, bf16[1168,128]{1,0:T(8,128)(2,1)S(1)}, u32[]{:S(2)}, u32[]{:S(2)}) collective-permute-start(bf16[1168,128]{1,0:T(8,128)(2,1)S(1)} %get-tuple-element.32.sent_left), channel_id=1, source_target_pairs={{15,0},{0,1},{1,2},{2,3},{3,4},{4,5},{5,6},{6,7},{7,8},{8,9},{9,10... | collective-permute-start | bytes 897032 | tf_op jit(solution)/shard_map/ppermute | solution.py:555
  18.5 17.3 %collective-permute-start.1 = (bf16[1168,128]{1,0:T(8,128)(2,1)S(1)}, bf16[1168,128]{1,0:T(8,128)(2,1)S(1)}, u32[]{:S(2)}, u32[]{:S(2)}) collective-permute-start(bf16[1168,128]{1,0:T(8,128)(2,1)S(1)} %get-tuple-element.36.sent_top), channel_id=1, source_target_pairs={{240,0},{0,16},{16,32},{32,48},{48,64},{64,80},{80,96},{96,112},{1... | collective-permute-start | bytes 897032 | tf_op jit(solution)/shard_map/ppermute | solution.py:555
  22.0 13.7 %copy-start.3 = (f32[1152,128]{1,0:T(8,128)S(1)}, f32[1152,128]{1,0:T(8,128)}, u32[]{:S(2)}) copy-start(f32[1152,128]{1,0:T(8,128)} %get-tuple-element.35.from_right) | copy-start | bytes 1769476
  22.1 13.7 %copy-start.4 = (bf16[128,1152]{1,0:T(8,128)(2,1)S(1)}, bf16[128,1152]{1,0:T(8,128)(2,1)}, u32[]{:S(2)}) copy-start(bf16[128,1152]{1,0:T(8,128)(2,1)} %get-tuple-element.49.right_pair) | copy-start | bytes 884740
  22.1 13.7 %copy-start.5 = (bf16[1152,128]{1,0:T(8,128)(2,1)S(1)}, bf16[1152,128]{1,0:T(8,128)(2,1)}, u32[]{:S(2)}) copy-start(bf16[1152,128]{1,0:T(8,128)(2,1)} %get-tuple-element.43.rows_t) | copy-start | bytes 884740
  22.1 13.7 %copy-start.10 = (bf16[96,96]{1,0:T(8,128)(2,1)S(1)}, bf16[96,96]{1,0:T(8,128)(2,1)}, u32[]{:S(2)}) copy-start(bf16[96,96]{1,0:T(8,128)(2,1)} %get-tuple-element.45.lay_a) | copy-start | bytes 55300
  22.1 13.7 %collective-permute-start = (bf16[1152,128]{1,0:T(8,128)(2,1)S(1)}, bf16[1152,128]{1,0:T(8,128)(2,1)S(1)}, u32[]{:S(2)}, u32[]{:S(2)}) collective-permute-start(bf16[1152,128]{1,0:T(8,128)(2,1)S(1)} %get-tuple-element.34), channel_id=1, source_target_pairs={{1,0},{2,1},{3,2},{4,3},{5,4},{6,5},{7,6},{8,7},{9,8},{10,9},{11,1... | collective-permute-start | bytes 884744 | tf_op jit(solution)/shard_map/ppermute | solution.py:555

commit v5 on v4

--- a/solution.py
+++ b/solution.py
@@ -157,7 +157,14 @@
             for a, b in pairs
         ]
 
-    return mask(leg_r, leg_u), mask(leg_d, leg_l), mask(leg_r, leg_d), mask(leg_u, leg_l)
+    return {
+        "ru": mask(leg_r, leg_u),
+        "dl": mask(leg_d, leg_l),
+        "rd": mask(leg_r, leg_d),
+        "ul": mask(leg_u, leg_l),
+        "dr": mask(leg_d, leg_r),
+        "lu": mask(leg_l, leg_u),
+    }
 
 
 def kept_rows(site, phys, virt, corner):
@@ -194,7 +201,7 @@
 
 
 def build_layers(kept, *wanted):
-    masks = dict(zip(("ru", "dl", "rd", "ul"), layer_masks()))
+    masks = layer_masks()
 
     for out, rows, cols in wanted:
         halves_of = []
@@ -241,8 +248,8 @@
 
 def right_kernel(
     phys_h, virt_h, site_h, corner_h, edge_h, edge_rows_h, sketches,
-    term, sent, pair_out, rows_out, lay_a, lay_b,
-    phys, virt, site, corner, edge, edge_rows, sketch, arrived, wide, thin, small,
+    term, sent, pair_out, cols_out, lay_b, lay_d,
+    phys, virt, site, corner, edge, edge_rows, sketch, arrived, wide, thin, small, rows_out, lay_a,
 ):
     copies = bring(
         (phys_h, virt_h, site_h, corner_h, edge_h, edge_rows_h, sketches.at[pl.ds(3 * CUT, CUT), :]),
@@ -254,8 +261,8 @@
     kept = kept_rows(site, phys, virt, small)
     for copy in copies[3:]:
         copy.wait()
-    build_layers(kept, (lay_a, "dl", "ru"), (lay_b, "ru", "dl"))
-    sent[CUT : CUT + 32, :] = jnp.zeros((32, CHI), BF16)
+    build_layers(kept, (lay_a, "dl", "ru"), (lay_b, "ru", "dl"), (lay_d, "dr", "lu"))
+    pack_rows(lambda p: jnp.transpose(slab(edge_rows, p).astype(F32)), wide, cols_out)
     corner_product((), corner, edge, edge_rows, sketch, lay_a, term, sent, pair_out, rows_out, wide, thin)
 
 
@@ -470,29 +477,29 @@
 
 
 def early_kernel(
-    from_lower, above_range, own_top, sent_top, beside,
-    above, top,
-    range_a, range_t,
+    from_lower, above_range, from_right, before_range,
+    above, before,
+    range_a, range_b,
 ):
     grams = [
         range_and_gram(from_lower, above_range, above_range, range_a),
-        range_and_gram(own_top, beside, sent_top, range_t),
+        range_and_gram(from_right, before_range, before_range, range_b),
     ]
     inverses = []
     run(eliminate(grams, inverses))
     above[...] = times_inverse(range_a[...], inverses[0]).astype(BF16)
-    top[...] = times_inverse(range_t[...], inverses[1]).astype(BF16)
+    before[...] = times_inverse(range_b[...], inverses[1]).astype(BF16)
 
 
 def late_kernel(
-    own_left, sent_left, below, from_right, before_range, above, top,
-    left_rows, rows_t, lay_c, lay_a, corner_edge, corner_side, lower_pair, right_pair,
+    own_left, sent_left, below, own_top, sent_top, beside, above, before,
+    left_rows, top_cols, lay_c, lay_d, corner_edge, corner_side, lower_pair, right_pair,
     out_lu, out_le, out_ll, out_tl, out_te, out_tr,
-    range_l, range_b, left, before, beside_a, beside_t, mixed_l, mixed_t, packed, wide, thin_l, thin_t,
+    range_l, range_t, left, top, beside_a, beside_b, mixed_l, mixed_t, packed, wide, thin_l, thin_t,
 ):
     grams = [
         range_and_gram(own_left, below, sent_left, range_l),
-        range_and_gram(from_right, before_range, before_range, range_b),
+        range_and_gram(own_top, beside, sent_top, range_t),
     ]
 
     def keep_l(rows, block):
@@ -502,28 +509,25 @@
         mixed_t[rows, :] = block
 
     def products():
-        beside_t[...] = side_by_side(top)
-        yield from chain(rows_t, beside_t, lay_a, thin_t, keep_t)
+        beside_b[...] = side_by_side(before)
+        yield from chain(top_cols, beside_b, lay_d, thin_t, keep_t)
         beside_a[...] = side_by_side(above)
         yield from chain(left_rows, beside_a, lay_c, thin_l, keep_l)
         out_lu[...] = unit(corner_from(above, corner_edge))
-        out_tr[...] = unit(corner_from(top, right_pair))
+        out_tl[...] = unit(jnp.transpose(corner_from(before, corner_side)))
 
     inverses = []
     weave(eliminate(grams, inverses), STEPS, products(), 2 * CHAIN_STEPS)
     left[...] = times_inverse(range_l[...], inverses[0]).astype(BF16)
-    before[...] = times_inverse(range_b[...], inverses[1]).astype(BF16)
+    top[...] = times_inverse(range_t[...], inverses[1]).astype(BF16)
     out_ll[...] = unit(corner_from(left, lower_pair))
-    out_tl[...] = unit(jnp.transpose(corner_from(before, corner_side)))
-    pack_rows(lambda p: slab(left, p), wide, packed)
-    result = unit(dot_tn(packed[...], mixed_l[...]))
-    for p in range(D2):
-        part = result[:, p * CHI : (p + 1) * CHI]
-        out_le[p * CHI : (p + 1) * CHI, :] = jnp.transpose(part)
-    pack_rows(lambda p: slab(before, p), wide, packed)
-    result = unit(dot_tn(packed[...], mixed_t[...]))
-    for p in range(D2):
-        out_te[p * CHI : (p + 1) * CHI, :] = result[:, p * CHI : (p + 1) * CHI]
+    out_tr[...] = unit(corner_from(top, right_pair))
+    for basis, mixed, out in ((left, mixed_l, out_le), (top, mixed_t, out_te)):
+        pack_rows(lambda p: slab(basis, p), wide, packed)
+        result = unit(dot_tn(packed[...], mixed[...]))
+        for p in range(D2):
+            part = result[:, p * CHI : (p + 1) * CHI]
+            out[p * CHI : (p + 1) * CHI, :] = jnp.transpose(part)
 
 
 def shape(*dims, dtype=BF16):
@@ -544,7 +548,7 @@
         ],
         out_specs=(whole,) * len(outs),
         scratch_shapes=scratch,
-        compiler_params=pltpu.CompilerParams(vmem_limit_bytes=VMEM if name != "right" else 60 * 1024 * 1024),
+        compiler_params=pltpu.CompilerParams(vmem_limit_bytes=VMEM if name != "upper" else 60 * 1024 * 1024),
         cost_estimate=pl.CostEstimate(flops=1, bytes_accessed=1, transcendentals=0),
     )(*ins)
 
@@ -586,11 +590,11 @@
     virt_s = pltpu.SMEM((3, 1, 4), jnp.int32)
     env_v = keep(2, CHI, dtype=jnp.int32)
     arrivals = lambda n: pltpu.SemaphoreType.DMA((n,))
-    from_right, sent_right, right_pair, rows_t, lay_a, lay_b = call(
+    from_right, sent_right, right_pair, top_cols, lay_b, lay_d = call(
         right_kernel, "right", [phys_charge, virt, site, ur, right, top, sketches],
-        [tall_wide, shape(CUT + 32, CHI), broad, tall, lay, lay],
+        [tall_wide, tall, broad, tall, lay, lay],
         [phys_s, virt_s, keep(27, 4, 3), keep(CHI, CHI), slabs, slabs, slabs, arrivals(7), wide, thin,
-         keep(216, CHI, dtype=F32)],
+         keep(216, CHI, dtype=F32), slabs, keep(LAY, LAY)],
         range(7),
     )
     beside = from_behind(sent_right, "lx", -1)
@@ -609,15 +613,15 @@
         range(1, 5),
     )
     below = from_behind(sent_lower, "ly", -1)
-    above, top_basis = call(
-        early_kernel, "early", [from_lower, above_range, own_top, sent_top, beside],
+    above, before = call(
+        early_kernel, "early", [from_lower, above_range, from_right, before_range],
         [tall, tall], [wide, wide],
     )
     square = keep(CUT, CUT)
     lu, le, lo, tl, te, tr = call(
         late_kernel, "late",
-        [own_left, sent_left, below, from_right, before_range, above, top_basis, left_rows, rows_t,
-         lay_c, lay_a, corner_edge, corner_side, lower_pair, right_pair],
+        [own_left, sent_left, below, own_top, sent_top, beside, above, before, left_rows, top_cols,
+         lay_c, lay_d, corner_edge, corner_side, lower_pair, right_pair],
         [corner, tall, corner, corner, tall, corner],
         [wide, wide, slabs, slabs, keep(CHI, CUT), keep(CHI, CUT), square, square, slabs, wide, thin, thin],
     )

time: 45.4 us -> 42.8 us (0.943)
  waiting for transfers between devices: 3.78 us -> 0.01 us
  Pallas kernels: 28.8 us -> 29.5 us
  starting transfers between devices: 11.6 us -> 12.2 us
    ppermute x4, waiting for transfers between devices: 3.78 us -> 0.01 us  [from_behind(): return lax.ppermute(block, axis, route)]
    pallas_call x5, Pallas kernels: 28.8 us -> 29.5 us  [call(): pl.pallas_call(body, name=name, out_shape=tuple(outs), in_specs=[pl.Block...]
    ppermute x4, starting transfers between devices: 11.6 us -> 12.2 us  [from_behind(): return lax.ppermute(block, axis, route)]
  transfers between devices with their start and end apart: 4 -> 4, of which waited for: 1 -> 0; matrix products, arithmetic and copies ran while one was open for 0% -> 0% of each run, Pallas kernels for 31% -> 31%
where the time goes in v5:
time: 42.8 us; the launch traced here: 42.7 us
  Pallas kernels  29.5 us (69%)
  starting transfers between devices  12.2 us (29%)
  between operations  0.92 us (2%)
    pallas_call x5, Pallas kernels, call(): pl.pallas_call(body, name=name, out_shape=tuple(outs), in_specs=[pl.Block...  29.5 us
    ppermute x4, starting transfers between devices, from_behind(): return lax.ppermute(block, axis, route)  12.2 us
  transfers between devices with their start and end apart: 4, of which 0 were waited for; matrix products, arithmetic and copies ran while one was open for 0% of the time, Pallas kernels for 31%

profile of v5, /device:TPU:8, one launch (start us, length us, event | category | flops | bytes accessed | tf_op | source)
XLA Modules:
  0.0 42.7 jit_solution(2116271235137798855)
XLA Ops:
  0.7 6.6 %upper.1 = (f32[1152,128]{1,0:T(8,128)}, f32[1152,128]{1,0:T(8,128)}, bf16[1168,128]{1,0:T(8,128)(2,1)}, bf16[1168,128]{1,0:T(8,128)(2,1)}, bf16[128,1152]{1,0:T...) custom-call(s32[1,1,4]{2,1,0:T(1,128)} %phys_h.3, ...), custom_call_target="tpu_custom_call" | custom-call | flops 1 | bytes 1 | tf_op jit(solution)/shard_map/upper/pallas_call | solution.py:542
  7.3 0.0 copy-start.2
  7.3 0.0 copy-start.11
  7.4 0.0 copy-start.14
  7.4 0.1 collective-permute-start.2
  7.5 2.0 %collective-permute-start.3 = (bf16[1168,128]{1,0:T(8,128)(2,1)}, bf16[1168,128]{1,0:T(8,128)(2,1)S(1)}, u32[]{:S(2)}, u32[]{:S(2)}) collective-permute-start(bf16[1168,128]{1,0:T(8,128)(2,1)} %get-tuple-element.36.sent_top), channel_id=1, source_target_pairs={{240,0},{0,16},{16,32},{32,48},{48,64},{64,80},{80,96},{96,112},{1... | collective-permute-start | bytes 897032 | tf_op jit(solution)/shard_map/ppermute | solution.py:559
  9.5 0.0 copy-done.17
  9.5 0.0 copy-done.12
  9.5 0.0 copy-done.10
  9.5 0.0 copy-done.13
  9.5 3.9 %right.1 = (f32[1152,128]{1,0:T(8,128)S(1)}, bf16[1152,128]{1,0:T(8,128)(2,1)S(1)}, bf16[128,1152]{1,0:T(8,128)(2,1)S(1)}, bf16[1152,128]{1,0:T(8,128)(2,1)S(1)}...) custom-call(s32[1,1,4]{2,1,0:T(1,128)S(1)} %copy-done.17, s32[3,1,4]{2,1,0:T(1,128)S(1)} %bitcast.59, ...), custom_call_target="tpu_custom_call" | custom-call | flops 1 | bytes 1 | tf_op jit(solution)/shard_map/right/pallas_call | solution.py:542
  13.4 6.0 %collective-permute-start.1 = (bf16[1152,128]{1,0:T(8,128)(2,1)S(1)}, bf16[1152,128]{1,0:T(8,128)(2,1)S(1)}, u32[]{:S(2)}, u32[]{:S(2)}) collective-permute-start(bf16[1152,128]{1,0:T(8,128)(2,1)S(1)} %get-tuple-element.37), channel_id=1, source_target_pairs={{16,0},{32,16},{48,32},{64,48},{80,64},{96,80},{112,96},{128,112},... | collective-permute-start | bytes 884744 | tf_op jit(solution)/shard_map/ppermute | solution.py:559
  19.4 0.0 copy-done.11
  19.4 0.0 copy-start.8
  19.4 3.2 %lower.1 = (f32[1152,128]{1,0:T(8,128)S(1)}, bf16[1152,128]{1,0:T(8,128)(2,1)S(1)}, bf16[128,1152]{1,0:T(8,128)(2,1)S(1)}) custom-call(bf16[96,96]{1,0:T(8,128)(2,1)S(1)} %get-tuple-element.33.layer, bf16[128,128]{1,0:T(8,128)(2,1)S(1)} %bitcast.57, bf16[1152,128]{1,0:T(8,128)(2,1)S(1)} %bitcast.53, bf16[1152,128]{1,0:T(8,128)(2,1)S(1)} %bitcast.51, ...), custom_call_target="tpu_custom_call" | custom-call | flops 1 | bytes 1 | tf_op jit(solution)/shard_map/lower/pallas_call | solution.py:542
  22.6 0.0 copy-start.3
  22.7 0.0 copy-start.15
  22.7 4.1 %collective-permute-start = (bf16[1152,128]{1,0:T(8,128)(2,1)S(1)}, bf16[1152,128]{1,0:T(8,128)(2,1)S(1)}, u32[]{:S(2)}, u32[]{:S(2)}) collective-permute-start(bf16[1152,128]{1,0:T(8,128)(2,1)S(1)} %get-tuple-element.34), channel_id=1, source_target_pairs={{1,0},{2,1},{3,2},{4,3},{5,4},{6,5},{7,6},{8,7},{9,8},{10,9},{11,1... | collective-permute-start | bytes 884744 | tf_op jit(solution)/shard_map/ppermute | solution.py:559
  26.8 0.0 collective-permute-done.2.above_range
  26.8 0.0 collective-permute-done.3.before_range
  26.8 6.2 %early.1 = (bf16[1152,128]{1,0:T(8,128)(2,1)S(1)}, bf16[1152,128]{1,0:T(8,128)(2,1)S(1)}) custom-call(f32[1152,128]{1,0:T(8,128)S(1)} %get-tuple-element.38.from_lower, bf16[1168,128]{1,0:T(8,128)(2,1)S(1)} %collective-permute-done.2.above_range, f32[1152,128]{1,0:T(8,128)S(1)} %get-tuple-element.39.from_right, ...), custom_call_target="tpu_custom_call" | custom-call | flops 1 | bytes 1 | tf_op jit(solution)/shard_map/early/pallas_call | solution.py:542
  33.1 0.0 collective-permute-done.1.beside
  33.1 0.0 collective-permute-done.below
  33.2 9.5 %late.1 = (bf16[128,128]{1,0:T(8,128)(2,1)}, bf16[1152,128]{1,0:T(8,128)(2,1)}, bf16[128,128]{1,0:T(8,128)(2,1)}, bf16[128,128]{1,0:T(8,128)(2,1)}, bf16[1152,128]{1,0:T(8,128)(2,1)}, /*index=5*/bf16[128,128]{1,0:T(8,128)(2,1)}) custom-call(f32[1152,128]{1,0:T(8,128)S(1)} %copy-done.3, bf16[1168,128]{1,0:T(8,128)(2,1)S(1)} %copy-done.5, ...), custom_call_target="tpu_custom_call" | custom-call | flops 1 | bytes 1 | tf_op jit(solution)/shard_map/late/pallas_call | solution.py:542
  (25 shorter events, 0.1 us)
Async XLA Ops:
  0.6 8.8 %copy-start.17 = (s32[1,1,4]{2,1,0:T(1,128)S(1)}, s32[1,1,4]{2,1,0:T(1,128)}, u32[]{:S(2)}) copy-start(s32[1,1,4]{2,1,0:T(1,128)} %phys_h.3) | copy-start | bytes 52
  0.6 8.8 %copy-start = (bf16[1,1,4,1152,128]{4,3,2,1,0:T(8,128)(2,1)S(1)}, bf16[1,1,4,1152,128]{4,3,2,1,0:T(8,128)(2,1)}, u32[]{:S(2)}) copy-start(bf16[1,1,4,1152,128]{4,3,2,1,0:T(8,128)(2,1)} %param.23) | copy-start | bytes 3538948
  0.7 8.8 %copy-start.1 = (bf16[1,1,128,9,128]{4,2,3,1,0:T(8,128)(2,1)S(1)}, bf16[1,1,128,9,128]{4,2,3,1,0:T(8,128)(2,1)}, u32[]{:S(2)}) copy-start(bf16[1,1,128,9,128]{4,2,3,1,0:T(8,128)(2,1)} %param.19) | copy-start | bytes 884740
  0.7 8.8 %copy-start.16 = (s32[1,1,4,3]{2,1,3,0:T(1,128)S(1)}, s32[1,1,4,3]{2,1,3,0:T(1,128)}, u32[]{:S(2)}) copy-start(s32[1,1,4,3]{2,1,3,0:T(1,128)} %param.14) | copy-start | bytes 148
  0.7 8.8 %copy-start.12 = (bf16[1,1,4,3,3,3,3]{6,2,5,4,3,1,0:T(4,128)(2,1)S(1)}, bf16[1,1,4,3,3,3,3]{6,2,5,4,3,1,0:T(4,128)(2,1)}, u32[]{:S(2)}) copy-start(bf16[1,1,4,3,3,3,3]{6,2,5,4,3,1,0:T(4,128)(2,1)} %param.12) | copy-start | bytes 1948
  0.7 8.8 %copy-start.10 = (bf16[1,1,128,9,128]{4,2,3,1,0:T(8,128)(2,1)S(1)}, bf16[1,1,128,9,128]{4,2,3,1,0:T(8,128)(2,1)}, u32[]{:S(2)}) copy-start(bf16[1,1,128,9,128]{4,2,3,1,0:T(8,128)(2,1)} %param.20) | copy-start | bytes 884740
  0.7 8.8 %copy-start.13 = (bf16[1,1,128,128]{3,2,1,0:T(8,128)(2,1)S(1)}, bf16[1,1,128,128]{3,2,1,0:T(8,128)(2,1)}, u32[]{:S(2)}) copy-start(bf16[1,1,128,128]{3,2,1,0:T(8,128)(2,1)} %param.17) | copy-start | bytes 98308
  7.3 12.0 %copy-start.2 = (bf16[1,1,128,9,128]{4,2,3,1,0:T(8,128)(2,1)S(1)}, bf16[1,1,128,9,128]{4,2,3,1,0:T(8,128)(2,1)}, u32[]{:S(2)}) copy-start(bf16[1,1,128,9,128]{4,2,3,1,0:T(8,128)(2,1)} %param.22) | copy-start | bytes 884740
  7.3 12.0 %copy-start.11 = (bf16[1,1,128,9,128]{4,2,3,1,0:T(8,128)(2,1)S(1)}, bf16[1,1,128,9,128]{4,2,3,1,0:T(8,128)(2,1)}, u32[]{:S(2)}) copy-start(bf16[1,1,128,9,128]{4,2,3,1,0:T(8,128)(2,1)} %param.21) | copy-start | bytes 884740
  7.4 12.0 %copy-start.14 = (bf16[1,1,128,128]{3,2,1,0:T(8,128)(2,1)S(1)}, bf16[1,1,128,128]{3,2,1,0:T(8,128)(2,1)}, u32[]{:S(2)}) copy-start(bf16[1,1,128,128]{3,2,1,0:T(8,128)(2,1)} %param.18) | copy-start | bytes 98308
  7.4 19.5 %collective-permute-start.2 = (bf16[1168,128]{1,0:T(8,128)(2,1)}, bf16[1168,128]{1,0:T(8,128)(2,1)S(1)}, u32[]{:S(2)}, u32[]{:S(2)}) collective-permute-start(bf16[1168,128]{1,0:T(8,128)(2,1)} %get-tuple-element.32.sent_left), channel_id=1, source_target_pairs={{15,0},{0,1},{1,2},{2,3},{3,4},{4,5},{5,6},{6,7},{7,8},{8,9},{9,10... | collective-permute-start | bytes 897032 | tf_op jit(solution)/shard_map/ppermute | solution.py:559
  7.5 19.4 %collective-permute-start.3 = (bf16[1168,128]{1,0:T(8,128)(2,1)}, bf16[1168,128]{1,0:T(8,128)(2,1)S(1)}, u32[]{:S(2)}, u32[]{:S(2)}) collective-permute-start(bf16[1168,128]{1,0:T(8,128)(2,1)} %get-tuple-element.36.sent_top), channel_id=1, source_target_pairs={{240,0},{0,16},{16,32},{32,48},{48,64},{64,80},{80,96},{96,112},{1... | collective-permute-start | bytes 897032 | tf_op jit(solution)/shard_map/ppermute | solution.py:559
  13.4 19.7 %collective-permute-start.1 = (bf16[1152,128]{1,0:T(8,128)(2,1)S(1)}, bf16[1152,128]{1,0:T(8,128)(2,1)S(1)}, u32[]{:S(2)}, u32[]{:S(2)}) collective-permute-start(bf16[1152,128]{1,0:T(8,128)(2,1)S(1)} %get-tuple-element.37), channel_id=1, source_target_pairs={{16,0},{32,16},{48,32},{64,48},{80,64},{96,80},{112,96},{128,112},... | collective-permute-start | bytes 884744 | tf_op jit(solution)/shard_map/ppermute | solution.py:559
  19.4 13.7 %copy-start.7 = (bf16[128,1152]{1,0:T(8,128)(2,1)S(1)}, bf16[128,1152]{1,0:T(8,128)(2,1)}, u32[]{:S(2)}) copy-start(bf16[128,1152]{1,0:T(8,128)(2,1)} %get-tuple-element.46.corner_edge) | copy-start | bytes 884740
  19.4 13.7 %copy-start.8 = (bf16[128,1152]{1,0:T(8,128)(2,1)S(1)}, bf16[128,1152]{1,0:T(8,128)(2,1)}, u32[]{:S(2)}) copy-start(bf16[128,1152]{1,0:T(8,128)(2,1)} %get-tuple-element.47.corner_side) | copy-start | bytes 884740
  19.4 13.7 %copy-start.9 = (bf16[1152,128]{1,0:T(8,128)(2,1)S(1)}, bf16[1152,128]{1,0:T(8,128)(2,1)}, u32[]{:S(2)}) copy-start(bf16[1152,128]{1,0:T(8,128)(2,1)} %get-tuple-element.42.left_rows) | copy-start | bytes 884740
  22.6 10.5 %copy-start.3 = (f32[1152,128]{1,0:T(8,128)S(1)}, f32[1152,128]{1,0:T(8,128)}, u32[]{:S(2)}) copy-start(f32[1152,128]{1,0:T(8,128)} %get-tuple-element.31.own_left) | copy-start | bytes 1769476
  22.6 10.5 %copy-start.4 = (f32[1152,128]{1,0:T(8,128)S(1)}, f32[1152,128]{1,0:T(8,128)}, u32[]{:S(2)}) copy-start(f32[1152,128]{1,0:T(8,128)} %get-tuple-element.35.own_top) | copy-start | bytes 1769476
  22.7 10.5 %copy-start.5 = (bf16[1168,128]{1,0:T(8,128)(2,1)S(1)}, bf16[1168,128]{1,0:T(8,128)(2,1)}, u32[]{:S(2)}) copy-start(bf16[1168,128]{1,0:T(8,128)(2,1)} %get-tuple-element.32.sent_left) | copy-start | bytes 897028
  22.7 10.5 %copy-start.6 = (bf16[1168,128]{1,0:T(8,128)(2,1)S(1)}, bf16[1168,128]{1,0:T(8,128)(2,1)}, u32[]{:S(2)}) copy-start(bf16[1168,128]{1,0:T(8,128)(2,1)} %get-tuple-element.36.sent_top) | copy-start | bytes 897028
  22.7 10.5 %copy-start.15 = (bf16[96,96]{1,0:T(8,128)(2,1)S(1)}, bf16[96,96]{1,0:T(8,128)(2,1)}, u32[]{:S(2)}) copy-start(bf16[96,96]{1,0:T(8,128)(2,1)} %get-tuple-element.44.lay_c) | copy-start | bytes 55300
  22.7 10.4 %collective-permute-start = (bf16[1152,128]{1,0:T(8,128)(2,1)S(1)}, bf16[1152,128]{1,0:T(8,128)(2,1)S(1)}, u32[]{:S(2)}, u32[]{:S(2)}) collective-permute-start(bf16[1152,128]{1,0:T(8,128)(2,1)S(1)} %get-tuple-element.34), channel_id=1, source_target_pairs={{1,0},{2,1},{3,2},{4,3},{5,4},{6,5},{7,6},{8,7},{9,8},{10,9},{11,1... | collective-permute-start | bytes 884744 | tf_op jit(solution)/shard_map/ppermute | solution.py:559
